TPU v7x, 256 devices: a whole 4x4x8 slice. The times are simulated.
256 devices in a mesh: owner: 64 (over z, x, core), helper: 4 (over y).
Axes of the slice: x: 4, y: 4, z: 8, core: 2. Of those that a mesh axis runs over, the one named last changes fastest.
Arguments:
- states: bfloat16 [128, 128, 768], P('owner'), may hold values from -6 to 6
- partners: int32 [128, 21], P('owner'), may hold values from -1 to 127, as said below
- self_proj: bfloat16 [3, 768, 768], P(None, None, 'helper'), may hold values from -0.28867513 to 0.28867513
- self_out: bfloat16 [768, 768], P('helper'), may hold values from -0.21875 to 0.21875
- cross_proj: bfloat16 [3, 768, 768], P(None, None, 'helper'), may hold values from -0.28867513 to 0.28867513
- cross_out: bfloat16 [768, 768], P('helper'), may hold values from -0.21875 to 0.21875
- gains: float32 [3, 768], replicated, may hold values from 0.5 to 1.5
Outputs:
- pair_states: bfloat16 [128, 21, 128, 768], P('owner', None, 'helper')
Inputs may be any that keep to these rules, and one draw needn't show every extreme that they name: Row i lists the images paired with image i, left-aligned, then -1 in the remaining slots. Pairs are symmetric. Images 2 * o and 2 * o + 1 belong to owner o. With M = 64 owners, every pair joins owner o with owner o + k modulo M for k from 1 to 10 or k = M // 2, or with owner o - k modulo M for k from 1 to 10; each of these 21 owners is joined to o by exactly one pair, so the two images of one owner take part in exactly 21 pairs together, and some image has 21 partners.
All inputs are finite; a program needn't handle non-finite values.
Results may differ from a plain program's by a relative error of at most 0.0095.
Values may be sent and summed in bfloat16 or wider, within the bound.
A program may use at most 128 MiB of HBM per device.

v0:
```python
import jax
import jax.numpy as jnp
from jax import lax
from jax.sharding import PartitionSpec as P

HEAD = 64


def norm_rows(values, gain_row):
    row_mean = jnp.mean(values, -1, keepdims=True)
    centred = values - row_mean
    row_var = jnp.mean(centred * centred, -1, keepdims=True)
    return centred * lax.rsqrt(row_var + 1e-05) * gain_row


def attend(queries, key_rows, value_rows):
    count_n, patch_n, column_n = queries.shape
    head_count = column_n // HEAD
    q_heads = queries.reshape(count_n, patch_n, head_count, HEAD)
    k_heads = key_rows.reshape(count_n, key_rows.shape[1], head_count, HEAD)
    v_heads = value_rows.reshape(count_n, value_rows.shape[1], head_count, HEAD)
    scores = jnp.einsum(
        "nqhe,nkhe->nhqk", q_heads, k_heads, preferred_element_type=jnp.float32
    ) * HEAD ** (-0.5)
    weights = jax.nn.softmax(scores, axis=-1).astype(jnp.bfloat16)
    context = jnp.einsum("nhqk,nkhe->nqhe", weights, v_heads, preferred_element_type=jnp.float32)
    return context.astype(jnp.bfloat16).reshape(count_n, patch_n, column_n)


def local(states, partners, self_proj, self_out, cross_proj, cross_out, gains):
    as_float = states.astype(jnp.float32)
    image_count, patch_count, model_width = states.shape
    normed = norm_rows(as_float, gains[0]).astype(jnp.bfloat16)
    key_norm = norm_rows(as_float, gains[2]).astype(jnp.bfloat16)
    cross_kv = jnp.einsum(
        "ipd,cdf->ipcf", key_norm, cross_proj[1:], preferred_element_type=jnp.float32
    ).astype(jnp.bfloat16)
    head_cols = cross_kv.shape[3]
    cross_kv = cross_kv.reshape(image_count, patch_count, 2 * head_cols)
    owner_count = lax.axis_size("owner")
    is_live = partners >= 0
    partner_owner = jnp.where(is_live, partners // image_count, -1)
    needed = jnp.any(
        partner_owner[:, :, None] == jnp.arange(owner_count, dtype=jnp.int32)[None, None, :], axis=1
    )
    slot_count = partners.shape[1]
    outgoing = jnp.einsum(
        "ed,epc->dpc", needed.astype(jnp.bfloat16), cross_kv, preferred_element_type=jnp.float32
    ).astype(jnp.bfloat16)
    incoming = lax.all_to_all(outgoing, "owner", split_axis=0, concat_axis=0, tiled=True)
    projected = jnp.einsum(
        "ipd,cdf->cipf", normed, self_proj, preferred_element_type=jnp.float32
    ).astype(jnp.bfloat16)
    context = attend(projected[0], projected[1], projected[2])
    own_heads = jnp.einsum("ipf,fd->ipd", context, self_out, preferred_element_type=jnp.float32)
    mixed = as_float + lax.psum(own_heads.astype(jnp.bfloat16), "helper").astype(jnp.float32)
    queries = jnp.einsum(
        "ipd,df->ipf",
        norm_rows(mixed, gains[1]).astype(jnp.bfloat16),
        cross_proj[0],
        preferred_element_type=jnp.float32,
    ).astype(jnp.bfloat16)
    flat_list = partners.reshape(-1)
    side_order = jnp.arange(image_count * slot_count, dtype=jnp.int32)
    side_partner = flat_list[side_order]
    side_image = side_order // slot_count
    side_live = side_partner >= 0
    sender = jnp.where(side_live, side_partner // image_count, 0)
    side_kv = incoming[sender]
    side_context = attend(queries[side_image], side_kv[:, :, :head_cols], side_kv[:, :, head_cols:])
    helper_count = lax.axis_size("helper")
    row_count = patch_count // helper_count
    row_start = lax.axis_index("helper") * row_count
    summed = lax.psum_scatter(
        jnp.einsum(
            "spf,fd->psd", side_context, cross_out, preferred_element_type=jnp.float32
        ).astype(jnp.bfloat16),
        "helper",
        scatter_dimension=0,
        tiled=True,
    ).astype(jnp.float32)
    cross_terms = jnp.transpose(summed, (1, 0, 2))
    own_rows = lax.dynamic_slice_in_dim(mixed, row_start, row_count, 1)
    result = (own_rows[side_image] + cross_terms).astype(jnp.bfloat16)
    result = jnp.where(side_live[:, None, None], result, jnp.zeros((), jnp.bfloat16))
    return result.reshape(image_count, slot_count, row_count, model_width)


def solution(mesh):
    return jax.shard_map(
        local,
        mesh=mesh,
        in_specs=(
            P("owner", None, None),
            P("owner", None),
            P(None, None, "helper"),
            P("helper", None),
            P(None, None, "helper"),
            P("helper", None),
            P(),
        ),
        out_specs=P("owner", None, "helper", None),
        check_vma=False,
    )
```

profile of v0, /device:TPU:1, one launch (start us, length us, event | category | flops | bytes accessed | tf_op | source)
XLA Modules:
  0.0 306.0 jit_solution(2265300305299333989)
XLA Ops:
  6.5 0.0 copy-start
  6.5 1.2 convert_reduce_fusion
  7.8 1.2 fusion.20
  9.0 0.9 slice_reduce_fusion
  9.9 1.6 convolution_convert_fusion.3
  11.5 0.2 copy.26
  11.7 0.7 compare_select_fusion.3
  12.4 0.1 fusion.42
  12.5 1.8 convolution_convert_fusion
  14.3 6.4 %copy.27 = bf16[64,128,384]{2,1,0:T(8,128)(2,1)} copy(bf16[64,128,384]{2,0,1:T(8,128)(2,1)S(1)} %convolution_convert_fusion) | data formatting | bytes 12582912 | tf_op jit(solution)/shard_map/convert_element_type | solution.py:49
  20.8 13.3 %all-to-all-start = ((bf16[64,128,384]{2,1,0:T(8,128)(2,1)}), bf16[64,128,384]{2,1,0:T(8,128)(2,1)}, u32[]{:S(2)}, u32[]{:S(2)}) async-start(bf16[64,128,384]{2,1,0:T(8,128)(2,1)} %copy.27), calls=%async_computation | async-start | bytes 12582912 | tf_op jit(solution)/shard_map/all_to_all | solution.py:50
  34.1 0.0 copy-start.3
  34.1 0.0 copy-start.5
  34.1 0.0 all-reduce.2.cloned.1.call-start
  34.1 0.0 copy-done
  34.1 0.0 copy-done.2
  34.2 0.5 fusion.12
  34.7 0.3 fusion.52
  35.1 0.3 convolution_multiply_fusion
  35.3 0.2 convolution_convert_fusion.5
  35.6 0.0 copy-done.3
  35.6 1.1 convolution_convert_fusion.1
  36.6 0.0 all-reduce.2.cloned.1.call-update
  36.7 0.2 reduce-scatter.2.cloned.1.call-start
  36.9 0.0 copy-done.5
  36.9 0.1 reshape.166
  37.0 0.8 gather_fusion
  37.8 46.6 %all-reduce.2.cloned.1.call-done = bf16[2,128,768]{2,1,0:T(8,128)(2,1)} async-done(((bf16[2,128,768]{2,1,0:T(8,128)(2,1)}), bf16[2,128,768]{2,1,0:T(8,128)(2,1)}) %all-reduce.2.cloned.1.call-update) | async-done | bytes 393232 | tf_op jit(solution)/shard_map/psum | solution.py:56
  84.5 1.2 fusion.49
  85.7 1.2 multiply_reduce_fusion.1
  86.9 1.5 convolution_convert_fusion.4
  88.4 0.9 gather_fusion.3
  89.3 83.3 %all-to-all-done = bf16[64,128,384]{2,1,0:T(8,128)(2,1)} async-done(((bf16[64,128,384]{2,1,0:T(8,128)(2,1)}), bf16[64,128,384]{2,1,0:T(8,128)(2,1)}, u32[]{:S(2)}, u32[]{:S(2)}) %all-to-all-start) | async-done | bytes 6291488 | tf_op jit(solution)/shard_map/all_to_all | solution.py:50
  172.6 6.2 %gather_fusion.2 = bf16[42,128,384]{2,1,0:T(8,128)(2,1)} fusion(bf16[64,128,384]{2,1,0:T(8,128)(2,1)} %all-to-all-done, s32[1024]{0:T(1024)S(1)} %pad_clamp_fusion), kind=kCustom, calls=%fused_computation.2 | custom fusion | bytes 8257704 | tf_op jit(solution)/shard_map/gather | solution.py:69
  178.8 6.7 %fusion.50 = (bf16[42,128,192]{2,1,0:T(8,128)(2,1)}, bf16[42,128,192]{2,1,0:T(8,128)(2,1)}) fusion(bf16[42,128,384]{2,1,0:T(8,128)(2,1)} %gather_fusion.2), kind=kLoop, calls=%fused_computation.97 | loop fusion | bytes 8257536 | tf_op jit(solution)/shard_map/slice | solution.py:70
  185.5 4.4 %copy.29 = bf16[42,128,192]{1,2,0:T(8,128)(2,1)} copy(bf16[42,128,192]{2,1,0:T(8,128)(2,1)} %get-tuple-element.8) | data formatting | bytes 4128768 | tf_op jit(solution)/shard_map/slice | solution.py:70
  189.8 4.3 %copy.28 = bf16[42,128,192]{1,2,0:T(8,128)(2,1)} copy(bf16[42,128,192]{2,1,0:T(8,128)(2,1)} %get-tuple-element.9) | data formatting | bytes 4128768 | tf_op jit(solution)/shard_map/slice | solution.py:70
  194.2 7.9 %fusion.53 = (f32[42,3,128]{2,1,0:T(4,128)S(1)}, f32[42,3,128,128]{2,3,1,0:T(8,128)}) fusion(bf16[42,128,3,64]{1,3,2,0:T(8,128)(2,1)S(1)} %bitcast.81, bf16[42,128,3,64]{1,3,2,0:T(8,128)(2,1)} %bitcast.82), kind=kOutput, calls=%fused_computation.100 | convolution fusion | flops 270434432 | bytes 12450816 | tf_op jit(solution)/shard_map/sub | solution.py:25
  202.1 0.0 copy-start.4
  202.1 5.2 %fusion.9 = bf16[42,3,64,128]{3,2,1,0:T(8,128)(2,1)S(1)} fusion(bf16[42,128,3,64]{1,3,2,0:T(8,128)(2,1)} %bitcast.83, f32[42,3,128,128]{2,3,1,0:T(8,128)} %get-tuple-element.16, f32[42,3,128]{2,1,0:T(4,128)S(1)} %get-tuple-element.15), kind=kOutput, calls=%fused_computation.17 | convolution fusion | flops 269402112 | bytes 12450816 | tf_op jit(solution)/shard_map/nhqk,nkhe->nqhe/dot_general | solution.py:26
  207.3 0.0 copy-done.4
  207.3 5.6 %convert_bitcast_fusion = bf16[128,42,768]{2,0,1:T(8,128)(2,1)} fusion(bf16[42,128,192]{1,2,0:T(8,128)(2,1)S(1)} %bitcast.84, bf16[192,768]{1,0:T(8,128)(2,1)S(1)} %copy-done.4), kind=kOutput, calls=%fused_computation.6 | convolution fusion | flops 1589575680 | bytes 10616832 | tf_op jit(solution)/shard_map/spf,fd->psd/dot_general | solution.py:75
  212.9 0.0 reduce-scatter.2.cloned.1.call-update
  213.0 0.0 copy-start.1
  213.0 2.8 gather_fusion.1
  215.8 78.5 %reduce-scatter.2.cloned.1.call-done = bf16[32,42,768]{2,0,1:T(8,128)(2,1)} async-done(((bf16[128,42,768]{2,0,1:T(8,128)(2,1)}), bf16[32,42,768]{2,0,1:T(8,128)(2,1)}) %reduce-scatter.2.cloned.1.call-update) | async-done | bytes 2064400 | tf_op jit(solution)/shard_map/reduce_scatter | solution.py:74
  294.3 4.9 %fusion.8 = bf16[42,32,768]{2,1,0:T(8,128)(2,1)} fusion(f32[42,32,768]{2,1,0:T(8,128)} %gather_fusion.1, bf16[32,42,768]{2,0,1:T(8,128)(2,1)} %reduce-scatter.2.cloned.1.call-done, pred[42]{0:T(512)(128)(4,1)S(1)} %broadcast_compare_fusion), kind=kLoop, calls=%fused_computation.16 | loop fusion | flops 4128768 | bytes 8257578 | tf_op jit(solution)/shard_map/jit(_where)/select_n | solution.py:85
  299.2 0.0 copy-done.1
  (14 shorter events, 0.1 us)
Async XLA Ops:
  6.5 27.6 %copy-start = (bf16[3,768,192]{1,2,0:T(8,128)(2,1)S(1)}, bf16[3,768,192]{1,2,0:T(8,128)(2,1)}, u32[]{:S(2)}) copy-start(bf16[3,768,192]{1,2,0:T(8,128)(2,1)} %param.9) | copy-start | bytes 2654212
  20.8 13.4 %copy-start.2 = (bf16[2,128,768]{2,1,0:T(8,128)(2,1)S(1)}, bf16[2,128,768]{2,1,0:T(8,128)(2,1)}, u32[]{:S(2)}) copy-start(bf16[2,128,768]{2,1,0:T(8,128)(2,1)} %param.7) | copy-start | bytes 1179652
  20.8 151.8 %all-to-all-start = ((bf16[64,128,384]{2,1,0:T(8,128)(2,1)}), bf16[64,128,384]{2,1,0:T(8,128)(2,1)}, u32[]{:S(2)}, u32[]{:S(2)}) async-start(bf16[64,128,384]{2,1,0:T(8,128)(2,1)} %copy.27), calls=%async_computation | async-start | bytes 12582912 | tf_op jit(solution)/shard_map/all_to_all | solution.py:50
  34.1 1.5 copy-start.3
  34.1 2.8 copy-start.5
  34.1 50.4 %all-reduce.2.cloned.1.call-start = ((), (), s32[]{:S(2)}) async-start(), calls=%async_computation.2 | async-start | bytes 786432 | tf_op jit(solution)/shard_map/psum | solution.py:56
  36.7 257.6 %reduce-scatter.2.cloned.1.call-start = ((), (), s32[]{:S(2)}) async-start(), calls=%async_computation.3 | async-start | bytes 10321920 | tf_op jit(solution)/shard_map/reduce_scatter | solution.py:74
  202.1 5.2 %copy-start.4 = (bf16[192,768]{1,0:T(8,128)(2,1)S(1)}, bf16[192,768]{1,0:T(8,128)(2,1)}, u32[]{:S(2)}) copy-start(bf16[192,768]{1,0:T(8,128)(2,1)} %param.12) | copy-start | bytes 884740
  213.0 86.2 %copy-start.1 = (bf16[3,768,192]{1,2,0:T(8,128)(2,1)S(1)}, bf16[3,768,192]{1,2,0:T(8,128)(2,1)}, u32[]{:S(2)}) copy-start(bf16[3,768,192]{1,2,0:T(8,128)(2,1)} %param.9) | copy-start | bytes 2654212
Sparse Core Ops, SparseCore 0:
  37.3 47.1 all-reduce.1
  213.0 81.1 reduce-scatter.1
where the time goes:
time: 307 us; the launch traced here: 306 us
  waiting for transfers between devices  208 us (68%)
  local copies, waits for them, and re-layouts  33.7 us (11%)
  matrix products  26.1 us (9%)
  between operations  13.6 us (4%)
  starting transfers between devices  13.5 us (4%)
  other arithmetic  10.6 us (3%)
    all_to_all x1, waiting for transfers between devices, local(): lax.all_to_all(outgoing, 'owner', split_axis=0, concat_axis=0, tiled=True)  83.3 us
    reduce_scatter x1, waiting for transfers between devices, local(): lax.psum_scatter(jnp.einsum('spf,fd->psd', side_context, cross_out, prefe...  78.5 us
    psum x1, waiting for transfers between devices, local(): lax.psum(own_heads.astype(jnp.bfloat16), 'helper').astype(jnp.float32)  46.6 us
    all_to_all x1, starting transfers between devices, local(): lax.all_to_all(outgoing, 'owner', split_axis=0, concat_axis=0, tiled=True)  13.3 us
    slice x2, local copies, waits for them, and re-layouts, local(): side_kv[:, :, :head_cols]  11 us
    sub x2, matrix products, attend(): weights = jax.nn.softmax(scores, axis=-1).astype(jnp.bfloat16)  8.26 us
    convert_element_type x1, local copies, waits for them, and re-layouts, local(): outgoing = jnp.einsum('ed,epc->dpc', needed.astype(jnp.bfloat16), cross_k...  6.43 us
    gather x1, local copies, waits for them, and re-layouts, local(): side_kv = incoming[sender]  6.21 us
  transfers between devices with their start and end apart: 3, of which 3 were waited for; matrix products, arithmetic and copies ran while one was open for 4% of the time, Pallas kernels for 0%

commit v1 on v0

v1 whole, which is shorter than its diff:
```python
import functools

import jax
import jax.numpy as jnp
from jax import lax
from jax.experimental import pallas as pl
from jax.experimental.pallas import tpu as pltpu
from jax.sharding import PartitionSpec as P

MESH = pl.DeviceIdType.MESH
BF16 = jnp.bfloat16
F32 = jnp.float32

OWNERS = 64
HELPERS = 4
IMAGES = 2
PATCHES = 128
ROWS = PATCHES // HELPERS
D = 768
HEAD = 64
HEADS = 3
COLS = HEADS * HEAD
SLOTS = 21
NEAR = 10
PAIRS = 11
LANES = 2 * COLS
PAD = 64
VMEM_LIMIT = 56 * 1024 * 1024


def dot(a, b):
    return jnp.dot(a, b, preferred_element_type=F32)


def dot_nt(a, b):
    return lax.dot_general(a, b, (((1,), (1,)), ((), ())), preferred_element_type=F32)


def pair_tiles(first, second):
    zero = jnp.zeros((first.shape[0], HEAD), F32)
    f = [first[:, HEAD * h : HEAD * (h + 1)] for h in range(HEADS)]
    s = [zero] * HEADS if second is None else [second[:, HEAD * h : HEAD * (h + 1)] for h in range(HEADS)]
    tiles = []
    for parity in range(2):
        row = []
        for h in range(HEADS):
            ordered = (s[h], f[h]) if (h + parity) % 2 == 0 else (f[h], s[h])
            row.append(jnp.concatenate(ordered, axis=1).astype(BF16))
        tiles.append(row)
    return tiles


def head_context(q_tile, kv_tile):
    scores = dot_nt(q_tile, kv_tile)
    top = jnp.max(scores, axis=1, keepdims=True)
    weights = jnp.exp(scores - top)
    total = jnp.sum(weights, axis=1, keepdims=True)
    return dot(weights.astype(BF16), kv_tile) * (1.0 / total)


def join_contexts(even, odd):
    low = lax.broadcasted_iota(jnp.int32, (PATCHES, 2 * HEAD), 1) < HEAD
    if odd is None:
        odd = [even[0], even[1], even[0]]
    return (
        jnp.where(low, even[0], even[1]).astype(BF16),
        jnp.where(low, even[2], odd[0]).astype(BF16),
        jnp.where(low, odd[1], odd[2]).astype(BF16),
    )


def exchange_kernel(
    part,
    states_hbm,
    sproj_hbm,
    sout_hbm,
    cproj_hbm,
    cout_hbm,
    gains,
    ctx_out,
    w_out,
    mixed_out,
    states_v,
    sproj_v,
    cproj_v,
    sw,
    x0,
    x2,
    kvbuf,
    sendbuf,
    recvbuf,
    sctx,
    mixed_v,
    qbuf,
    ctxbuf,
    bits,
    in_sem,
    loc_sem,
    own_sem,
    kv_send,
    kv_recv,
    w_send,
    w_recv,
    f_send,
    f_recv,
    s_send,
    s_recv,
    c_send,
    c_recv,
):
    me = lax.axis_index("owner")
    my_h = lax.axis_index("helper")
    core = me % 2
    sibling = me + 1 - 2 * core

    def owner_at(offset):
        return (me + offset + OWNERS) % OWNERS

    def helper_at(step):
        return (my_h + step) % HELPERS

    barrier = pltpu.get_barrier_semaphore()

    @pl.loop(0, NEAR)
    def _(k):
        for sign in (1, -1):
            pl.semaphore_signal(
                barrier, inc=1, device_id=(owner_at(sign * (k + 1)), my_h), device_id_type=MESH
            )

    pl.semaphore_signal(barrier, inc=1, device_id=(owner_at(32), my_h), device_id_type=MESH)
    for step in range(1, HELPERS):
        pl.semaphore_signal(barrier, inc=1, device_id=(me, helper_at(step)), device_id_type=MESH)

    loads = [
        pltpu.make_async_copy(states_hbm, states_v, in_sem.at[0]),
        pltpu.make_async_copy(cproj_hbm, cproj_v, in_sem.at[1]),
        pltpu.make_async_copy(sproj_hbm, sproj_v, in_sem.at[2]),
        pltpu.make_async_copy(sout_hbm, sw.at[my_h, pl.ds(PAD, COLS)], in_sem.at[3]),
        pltpu.make_async_copy(cout_hbm, w_out.at[my_h], in_sem.at[4]),
    ]
    for load in loads:
        load.start()
    sw[:, 0:PAD] = jnp.zeros((HELPERS, PAD, D), BF16)
    sw[:, PAD + COLS :] = jnp.zeros((HELPERS, PAD, D), BF16)

    @pl.loop(0, SLOTS)
    def _(j):
        offset = jnp.where(j == SLOTS - 1, 32, (1 + j // 2) * (1 - 2 * (j % 2)))
        target = owner_at(offset)
        bit = jnp.int32(0)
        for s in range(SLOTS):
            p = part[1, s]
            hit = jnp.logical_and(p >= 2 * target, p <= 2 * target + 1)
            bit = jnp.where(hit, 1, bit)
        bits[j] = bit

    loads[0].wait()
    as_float = states_v[...].reshape(IMAGES * PATCHES, D).astype(F32)
    row_mean = jnp.mean(as_float, -1, keepdims=True)
    centred = as_float - row_mean
    row_var = jnp.mean(centred * centred, -1, keepdims=True)
    scaled = centred * lax.rsqrt(row_var + 1e-05)
    x2[...] = (scaled * gains[2:3, :]).astype(BF16)
    x0[...] = (scaled * gains[0:1, :]).astype(BF16)

    loads[1].wait()
    key_rows = dot(x2[...], cproj_v[1])
    value_rows = dot(x2[...], cproj_v[2])
    tiles = pair_tiles(key_rows, value_rows)
    for parity in range(2):
        for h in range(HEADS):
            for image in range(IMAGES):
                kvbuf[parity, image, :, 128 * h : 128 * (h + 1)] = tiles[parity][h][
                    PATCHES * image : PATCHES * (image + 1)
                ]

    pl.semaphore_wait(barrier, SLOTS + HELPERS - 1)

    def half(owner_core):
        return pl.ds(pl.multiple_of(owner_core * (COLS // 2), COLS // 2), COLS // 2)

    def self_rows(h, owner_core):
        return sw.at[h, pl.ds(pl.multiple_of(PAD + owner_core * (COLS // 2), 32), COLS // 2)]

    def weight_copy(which, step):
        source = sout_hbm if which == 0 else cout_hbm
        landing = self_rows(my_h, core) if which == 0 else w_out.at[my_h, half(core)]
        return pltpu.make_async_remote_copy(
            src_ref=source.at[half(core)],
            dst_ref=landing,
            send_sem=w_send.at[which, step - 1],
            recv_sem=w_recv.at[which, step - 1],
            device_id=(me, helper_at(step)),
            device_id_type=MESH,
        )

    def forward_copy(which, step):
        source = helper_at(HELPERS - step)
        block = self_rows(source, core) if which == 0 else w_out.at[source, half(core)]
        return pltpu.make_async_remote_copy(
            src_ref=block,
            dst_ref=block,
            send_sem=f_send.at[which, step - 1],
            recv_sem=f_recv.at[which, step - 1],
            device_id=(sibling, my_h),
            device_id_type=MESH,
        )

    def kv_copy(j, offset, landing):
        return pltpu.make_async_remote_copy(
            src_ref=sendbuf.at[j],
            dst_ref=recvbuf.at[landing],
            send_sem=kv_send.at[j],
            recv_sem=kv_recv.at[landing],
            device_id=(owner_at(offset), my_h),
            device_id_type=MESH,
        )

    for step in range(1, HELPERS):
        weight_copy(0, step).start()

    kv_copy_last = kv_copy(SLOTS - 1, 32, SLOTS - 1)
    sendbuf[SLOTS - 1] = kvbuf[0, bits[SLOTS - 1]]
    kv_copy_last.start()

    @pl.loop(0, NEAR)
    def _(k):
        sendbuf[2 * k] = kvbuf[1, bits[2 * k]]
        kv_copy(2 * k, k + 1, 2 * k + 1).start()
        sendbuf[2 * k + 1] = kvbuf[0, bits[2 * k + 1]]
        kv_copy(2 * k + 1, -(k + 1), 2 * k).start()

    for step in range(1, HELPERS):
        weight_copy(1, step).start()

    loads[2].wait()
    sq = dot(x0[...], sproj_v[0]) * HEAD ** (-0.5)
    sk = dot(x0[...], sproj_v[1])
    sv = dot(x0[...], sproj_v[2])
    q_tiles = pair_tiles(sq, None)
    kv_tiles = pair_tiles(sk, sv)
    contexts = []
    for image in range(IMAGES):
        rows = slice(PATCHES * image, PATCHES * (image + 1))
        contexts.append(
            [head_context(q_tiles[image][h][rows], kv_tiles[image][h][rows]) for h in range(HEADS)]
        )
    for t, tile in enumerate(join_contexts(*contexts)):
        sctx[my_h, :, 128 * t : 128 * (t + 1)] = tile

    def self_copy(step):
        return pltpu.make_async_remote_copy(
            src_ref=sctx.at[my_h],
            dst_ref=sctx.at[my_h],
            send_sem=s_send.at[step - 1],
            recv_sem=s_recv.at[step - 1],
            device_id=(me, helper_at(step)),
            device_id_type=MESH,
        )

    def self_arrival(step):
        source = helper_at(HELPERS - step)
        return pltpu.make_async_remote_copy(
            src_ref=sctx.at[source],
            dst_ref=sctx.at[source],
            send_sem=s_send.at[step - 1],
            recv_sem=s_recv.at[step - 1],
            device_id=(me, source),
            device_id_type=MESH,
        )

    def weight_arrival(which, step):
        source = helper_at(HELPERS - step)
        landed = self_rows(source, core) if which == 0 else w_out.at[source, half(core)]
        return pltpu.make_async_remote_copy(
            src_ref=landed,
            dst_ref=landed,
            send_sem=w_send.at[which, step - 1],
            recv_sem=w_recv.at[which, step - 1],
            device_id=(me, source),
            device_id_type=MESH,
        )

    def forward_arrival(which, step):
        source = helper_at(HELPERS - step)
        landed = self_rows(source, 1 - core) if which == 0 else w_out.at[source, half(1 - core)]
        return pltpu.make_async_remote_copy(
            src_ref=landed,
            dst_ref=landed,
            send_sem=f_send.at[which, step - 1],
            recv_sem=f_recv.at[which, step - 1],
            device_id=(sibling, my_h),
            device_id_type=MESH,
        )

    for step in range(1, HELPERS):
        self_copy(step).start()
    for step in range(1, HELPERS):
        weight_arrival(0, step).wait_recv()
        forward_copy(0, step).start()
    for step in range(1, HELPERS):
        forward_arrival(0, step).wait_recv()
    for step in range(1, HELPERS):
        self_arrival(step).wait_recv()
    loads[3].wait()

    for image in range(IMAGES):
        total = states_v[image].astype(F32)
        for h in range(HELPERS):
            if image == 0:
                total += dot(sctx[h, :, 0:256], sw[h, PAD:])
            else:
                total += dot(sctx[h, :, 128:384], sw[h, 0 : PAD + COLS])
        mixed_v[image] = total
        row_mean = jnp.mean(total, -1, keepdims=True)
        centred = total - row_mean
        row_var = jnp.mean(centred * centred, -1, keepdims=True)
        x0[PATCHES * image : PATCHES * (image + 1)] = (
            centred * lax.rsqrt(row_var + 1e-05) * gains[1:2, :]
        ).astype(BF16)

    def my_rows(helper):
        return pl.ds(pl.multiple_of(helper * ROWS, ROWS), ROWS)

    mixed_copy = pltpu.make_async_copy(mixed_v.at[:, my_rows(my_h)], mixed_out, loc_sem.at[0])
    mixed_copy.start()

    queries = dot(x0[...], cproj_v[0]) * HEAD ** (-0.5)
    q_tiles = pair_tiles(queries, None)
    for parity in range(2):
        for h in range(HEADS):
            for image in range(IMAGES):
                qbuf[parity, image, h] = q_tiles[parity][h][PATCHES * image : PATCHES * (image + 1)]

    def context_copy(pair, step):
        return pltpu.make_async_remote_copy(
            src_ref=ctxbuf.at[pair, my_rows(helper_at(step))],
            dst_ref=ctx_out.at[my_h, pair],
            send_sem=c_send.at[pair, step - 1],
            recv_sem=c_recv.at[pair, step - 1],
            device_id=(me, helper_at(step)),
            device_id_type=MESH,
        )

    def context_arrival(pair, step):
        source = helper_at(HELPERS - step)
        return pltpu.make_async_remote_copy(
            src_ref=ctxbuf.at[pair, my_rows(my_h)],
            dst_ref=ctx_out.at[source, pair],
            send_sem=c_send.at[pair, step - 1],
            recv_sem=c_recv.at[pair, step - 1],
            device_id=(me, source),
            device_id_type=MESH,
        )

    def own_copy(pair):
        return pltpu.make_async_copy(
            ctxbuf.at[pair, my_rows(my_h)], ctx_out.at[my_h, pair], own_sem.at[pair]
        )

    def kv_arrival(j, offset):
        return pltpu.make_async_remote_copy(
            src_ref=sendbuf.at[j],
            dst_ref=recvbuf.at[j],
            send_sem=kv_send.at[j],
            recv_sem=kv_recv.at[j],
            device_id=(owner_at(offset), my_h),
            device_id_type=MESH,
        )

    def slot_contexts(j, parity):
        image = bits[j]
        return [
            head_context(qbuf[parity, image, h], recvbuf[j, :, 128 * h : 128 * (h + 1)])
            for h in range(HEADS)
        ]

    def finish_pair(pair, even, odd):
        for t, tile in enumerate(join_contexts(even, odd)):
            ctxbuf[pair, :, 128 * t : 128 * (t + 1)] = tile
        for step in range(1, HELPERS):
            context_copy(pair, step).start()
        own_copy(pair).start()

    @pl.loop(0, NEAR)
    def _(pair):
        kv_arrival(2 * pair, pair + 1).wait_recv()
        even = slot_contexts(2 * pair, 0)
        kv_arrival(2 * pair + 1, -(pair + 1)).wait_recv()
        odd = slot_contexts(2 * pair + 1, 1)
        finish_pair(pair, even, odd)

    kv_arrival(SLOTS - 1, 32).wait_recv()
    finish_pair(PAIRS - 1, slot_contexts(SLOTS - 1, 0), None)

    for step in range(1, HELPERS):
        weight_arrival(1, step).wait_recv()
        forward_copy(1, step).start()
    for step in range(1, HELPERS):
        forward_arrival(1, step).wait_recv()
    loads[4].wait()
    mixed_copy.wait()
    for step in range(1, HELPERS):
        self_copy(step).wait_send()
        for which in range(2):
            weight_copy(which, step).wait_send()
            forward_copy(which, step).wait_send()

    @pl.loop(0, NEAR)
    def _(k):
        kv_copy(2 * k, k + 1, 2 * k + 1).wait_send()
        kv_copy(2 * k + 1, -(k + 1), 2 * k).wait_send()

    kv_copy_last.wait_send()

    @pl.loop(0, PAIRS)
    def _(pair):
        for step in range(1, HELPERS):
            context_copy(pair, step).wait_send()
            context_arrival(pair, step).wait_recv()
        own_copy(pair).wait()


def place_kernel(
    part, ctx_hbm, w_hbm, mixed, out, ctx, w, terms, result, blank, ctx_sem, w_sem, out_sem
):
    me = lax.axis_index("owner")
    load_w = pltpu.make_async_copy(w_hbm, w.at[:, pl.ds(PAD, COLS)], w_sem)
    load_ctx = pltpu.make_async_copy(ctx_hbm, ctx, ctx_sem)
    load_w.start()
    load_ctx.start()
    w[:, 0:PAD] = jnp.zeros((HELPERS, PAD, D), BF16)
    w[:, PAD + COLS :] = jnp.zeros((HELPERS, PAD, D), BF16)
    blank[...] = jnp.zeros((ROWS, D), BF16)
    load_w.wait()
    load_ctx.wait()
    for parity in range(2):
        total = None
        for h in range(HELPERS):
            if parity == 0:
                term = dot(ctx[h, :, :, 0:256].reshape(PAIRS * ROWS, 256), w[h, PAD:])
            else:
                term = dot(ctx[h, :, :, 128:384].reshape(PAIRS * ROWS, 256), w[h, 0 : PAD + COLS])
            total = term if total is None else total + term
        terms[parity] = total.reshape(PAIRS, ROWS, D)

    def out_copy(source, image, slot):
        return pltpu.make_async_copy(source, out.at[image, slot], out_sem.at[image, slot])

    for image in range(IMAGES):

        @pl.loop(0, SLOTS)
        def _(slot):
            p = part[image, slot]
            offset = (lax.div(jnp.maximum(p, 0), 2) - me + OWNERS) % OWNERS
            far = offset == 32
            back = offset > 32
            pair = jnp.where(far, PAIRS - 1, jnp.where(back, OWNERS - offset, offset) - 1)
            pair = jnp.clip(pair, 0, PAIRS - 1)
            parity = jnp.where(back, 1, 0)

            @pl.when(p >= 0)
            def _():
                result[image, slot] = (terms[parity, pair] + mixed[image]).astype(BF16)
                out_copy(result.at[image, slot], image, slot).start()

            @pl.when(p < 0)
            def _():
                out_copy(blank, image, slot).start()

    for image in range(IMAGES):

        @pl.loop(0, SLOTS)
        def _(slot):
            out_copy(blank, image, slot).wait()


def local(states, partners, self_proj, self_out, cross_proj, cross_out, gains):
    any_spec = pl.BlockSpec(memory_space=pl.ANY)
    smem = pl.BlockSpec(memory_space=pltpu.SMEM)
    vmem = pl.BlockSpec(memory_space=pltpu.VMEM)
    dma = pltpu.SemaphoreType.DMA
    ctx, weight, mixed = pl.pallas_call(
        exchange_kernel,
        out_shape=(
            jax.ShapeDtypeStruct((HELPERS, PAIRS, ROWS, LANES), BF16),
            jax.ShapeDtypeStruct((HELPERS, COLS, D), BF16),
            jax.ShapeDtypeStruct((IMAGES, ROWS, D), F32),
        ),
        in_specs=[smem, any_spec, any_spec, any_spec, any_spec, any_spec, vmem],
        out_specs=(any_spec, any_spec, any_spec),
        scratch_shapes=[
            pltpu.VMEM((IMAGES, PATCHES, D), BF16),
            pltpu.VMEM((3, D, COLS), BF16),
            pltpu.VMEM((3, D, COLS), BF16),
            pltpu.VMEM((HELPERS, COLS + 2 * PAD, D), BF16),
            pltpu.VMEM((IMAGES * PATCHES, D), BF16),
            pltpu.VMEM((IMAGES * PATCHES, D), BF16),
            pltpu.VMEM((2, IMAGES, PATCHES, LANES), BF16),
            pltpu.VMEM((SLOTS, PATCHES, LANES), BF16),
            pltpu.VMEM((SLOTS, PATCHES, LANES), BF16),
            pltpu.VMEM((HELPERS, PATCHES, LANES), BF16),
            pltpu.VMEM((IMAGES, PATCHES, D), F32),
            pltpu.VMEM((2, IMAGES, HEADS, PATCHES, 2 * HEAD), BF16),
            pltpu.VMEM((PAIRS, PATCHES, LANES), BF16),
            pltpu.SMEM((SLOTS,), jnp.int32),
            dma((5,)),
            dma((1,)),
            dma((PAIRS,)),
            dma((SLOTS,)),
            dma((SLOTS,)),
            dma((2, 3)),
            dma((2, 3)),
            dma((2, 3)),
            dma((2, 3)),
            dma((3,)),
            dma((3,)),
            dma((PAIRS, 3)),
            dma((PAIRS, 3)),
        ],
        compiler_params=pltpu.CompilerParams(
            collective_id=0, has_side_effects=True, vmem_limit_bytes=VMEM_LIMIT
        ),
        name="exchange",
    )(partners, states, self_proj, self_out, cross_proj, cross_out, gains)
    return pl.pallas_call(
        place_kernel,
        out_shape=jax.ShapeDtypeStruct((IMAGES, SLOTS, ROWS, D), BF16),
        in_specs=[smem, any_spec, any_spec, vmem],
        out_specs=any_spec,
        scratch_shapes=[
            pltpu.VMEM((HELPERS, PAIRS, ROWS, LANES), BF16),
            pltpu.VMEM((HELPERS, COLS + 2 * PAD, D), BF16),
            pltpu.VMEM((2, PAIRS, ROWS, D), F32),
            pltpu.VMEM((IMAGES, SLOTS, ROWS, D), BF16),
            pltpu.VMEM((ROWS, D), BF16),
            dma,
            dma,
            dma((IMAGES, SLOTS)),
        ],
        compiler_params=pltpu.CompilerParams(vmem_limit_bytes=VMEM_LIMIT),
        name="place",
    )(partners, ctx, weight, mixed)


def solution(mesh):
    return jax.shard_map(
        local,
        mesh=mesh,
        in_specs=(
            P("owner", None, None),
            P("owner", None),
            P(None, None, "helper"),
            P("helper", None),
            P(None, None, "helper"),
            P("helper", None),
            P(),
        ),
        out_specs=P("owner", None, "helper", None),
        check_vma=False,
    )
```

time: 307 us -> 65.4 us (0.21)
  waiting for transfers between devices: 208 us -> 0 us
  Pallas kernels: 0 us -> 61.4 us
  local copies, waits for them, and re-layouts: 33.7 us -> 3.82 us
  matrix products: 26.1 us -> 0 us
  between operations: 13.6 us -> 0.01 us
  starting transfers between devices: 13.5 us -> 0 us
  other arithmetic: 10.6 us -> 0 us
    all_to_all x1 -> x0, waiting for transfers between devices: 83.3 us -> none  [local(): lax.all_to_all(outgoing, 'owner', split_axis=0, concat_axis=0, tiled=True)]
    reduce_scatter x1 -> x0, waiting for transfers between devices: 78.5 us -> none  [local(): lax.psum_scatter(jnp.einsum('spf,fd->psd', side_context, cross_out, prefe...]
    pallas_call x0 -> x2, Pallas kernels: none -> 61.4 us  [the longest x1 55.3 us: local(): pl.pallas_call(exchange_kernel, out_shape=(jax.ShapeDtypeStruct((HELPERS,...]
    psum x1 -> x0, waiting for transfers between devices: 46.6 us -> none  [local(): lax.psum(own_heads.astype(jnp.bfloat16), 'helper').astype(jnp.float32)]
    dot_general x9 -> x0, matrix products: 17.8 us -> none  [the longest x1 5.56 us: local(): jnp.einsum('spf,fd->psd', side_context, cross_out, preferred_element_type...]
    slice x5 -> x0, local copies, waits for them, and re-layouts: 16.2 us -> none  [the longest x2 11 us: local(): side_kv[:, :, :head_cols]]
    all_to_all x1 -> x0, starting transfers between devices: 13.3 us -> none  [local(): lax.all_to_all(outgoing, 'owner', split_axis=0, concat_axis=0, tiled=True)]
    gather x4 -> x0, local copies, waits for them, and re-layouts: 10.7 us -> none  [the longest x1 6.21 us: local(): side_kv = incoming[sender]]
  transfers between devices with their start and end apart: 3 -> 0, of which waited for: 3 -> 0; matrix products, arithmetic and copies ran while one was open for 4% -> 0% of each run, Pallas kernels for 0% -> 0%
where the time goes in v1:
time: 65.4 us; the launch traced here: 65.2 us
  Pallas kernels  61.4 us (94%)
  local copies, waits for them, and re-layouts  3.82 us (6%)
    pallas_call x1, Pallas kernels, local(): pl.pallas_call(exchange_kernel, out_shape=(jax.ShapeDtypeStruct((HELPERS,...  55.3 us
    pallas_call x1, Pallas kernels, local(): pl.pallas_call(place_kernel, out_shape=jax.ShapeDtypeStruct((IMAGES, SLOT...  6.11 us
    unnamed x4, local copies, waits for them, and re-layouts  3.82 us

profile of v1, /device:TPU:1, one launch (start us, length us, event | category | flops | bytes accessed | tf_op | source)
XLA Modules:
  0.0 65.2 jit_solution(22558922161104778)
XLA Ops:
  0.0 0.0 copy-start
  0.0 2.4 %copy.8.sproj_hbm = bf16[3,768,192]{2,1,0:T(8,128)(2,1)} copy(bf16[3,768,192]{1,2,0:T(8,128)(2,1)} %param.9) | data formatting | bytes 1769472 | tf_op args[2]
  2.4 0.0 copy-done
  2.4 1.4 %copy.9.cproj_hbm = bf16[3,768,192]{2,1,0:T(8,128)(2,1)} copy(bf16[3,768,192]{1,2,0:T(8,128)(2,1)S(1)} %copy-done) | data formatting | bytes 1769472 | tf_op args[4]
  3.8 55.3 %exchange.1 = (bf16[4,11,32,384]{3,2,1,0:T(8,128)(2,1)}, bf16[4,192,768]{2,1,0:T(8,128)(2,1)}, f32[2,32,768]{2,1,0:T(8,128)}) custom-call(s32[2,21]{1,0:T(2,128)} %part.3, bf16[2,128,768]{2,1,0:T(8,128)(2,1)} %states_hbm.1, bf16[3,768,192]{2,1,0:T(8,128)(2,1)} %copy.8.sproj_hbm, bf16[192,768]{1,0:T(8,128)(2,1)} %sout_hbm.1, ...), custom_call_target="tpu_custom_call" | custom-call | tf_op jit(solution)/shard_map/exchange/pallas_call | solution.py:484
  59.1 6.1 %place.1 = bf16[2,21,32,768]{3,2,1,0:T(8,128)(2,1)} custom-call(s32[2,21]{1,0:T(2,128)} %part.3, bf16[4,11,32,384]{3,2,1,0:T(8,128)(2,1)} %get-tuple-element.8.ctx_hbm, bf16[4,192,768]{2,1,0:T(8,128)(2,1)} %get-tuple-element.9.w_hbm, f32[2,32,768]{2,1,0:T(8,128)} %get-tuple-element.10.mixed), custom_call_target="tpu_custom_call" | custom-call | tf_op jit(solution)/shard_map/place/pallas_call | solution.py:527
Async XLA Ops:
  0.0 2.4 %copy-start = (bf16[3,768,192]{1,2,0:T(8,128)(2,1)S(1)}, bf16[3,768,192]{1,2,0:T(8,128)(2,1)}, u32[]{:S(2)}) copy-start(bf16[3,768,192]{1,2,0:T(8,128)(2,1)} %param.11) | copy-start | bytes 2654212

commit v2 on v1

--- a/solution.py
+++ b/solution.py
@@ -50,12 +50,13 @@
     return tiles
 
 
-def head_context(q_tile, kv_tile):
-    scores = dot_nt(q_tile, kv_tile)
-    top = jnp.max(scores, axis=1, keepdims=True)
-    weights = jnp.exp(scores - top)
-    total = jnp.sum(weights, axis=1, keepdims=True)
-    return dot(weights.astype(BF16), kv_tile) * (1.0 / total)
+def head_contexts(tiles):
+    scores = [dot_nt(q, kv) for q, kv in tiles]
+    weights = [jnp.exp(s - jnp.max(s, axis=1, keepdims=True)) for s in scores]
+    totals = [jnp.sum(w, axis=1, keepdims=True) for w in weights]
+    return [
+        dot(w.astype(BF16), kv) * (1.0 / t) for w, t, (_, kv) in zip(weights, totals, tiles)
+    ]
 
 
 def join_contexts(even, odd):
@@ -165,8 +166,8 @@
     x0[...] = (scaled * gains[0:1, :]).astype(BF16)
 
     loads[1].wait()
-    key_rows = dot(x2[...], cproj_v[1])
-    value_rows = dot(x2[...], cproj_v[2])
+    key_rows = dot_nt(x2[...], cproj_v[1])
+    value_rows = dot_nt(x2[...], cproj_v[2])
     tiles = pair_tiles(key_rows, value_rows)
     for parity in range(2):
         for h in range(HEADS):
@@ -235,18 +236,20 @@
         weight_copy(1, step).start()
 
     loads[2].wait()
-    sq = dot(x0[...], sproj_v[0]) * HEAD ** (-0.5)
-    sk = dot(x0[...], sproj_v[1])
-    sv = dot(x0[...], sproj_v[2])
+    sq = dot_nt(x0[...], sproj_v[0]) * HEAD ** (-0.5)
+    sk = dot_nt(x0[...], sproj_v[1])
+    sv = dot_nt(x0[...], sproj_v[2])
     q_tiles = pair_tiles(sq, None)
     kv_tiles = pair_tiles(sk, sv)
-    contexts = []
-    for image in range(IMAGES):
-        rows = slice(PATCHES * image, PATCHES * (image + 1))
-        contexts.append(
-            [head_context(q_tiles[image][h][rows], kv_tiles[image][h][rows]) for h in range(HEADS)]
-        )
-    for t, tile in enumerate(join_contexts(*contexts)):
+    pieces = [slice(PATCHES * image, PATCHES * (image + 1)) for image in range(IMAGES)]
+    contexts = head_contexts(
+        [
+            (q_tiles[image][h][pieces[image]], kv_tiles[image][h][pieces[image]])
+            for image in range(IMAGES)
+            for h in range(HEADS)
+        ]
+    )
+    for t, tile in enumerate(join_contexts(contexts[:HEADS], contexts[HEADS:])):
         sctx[my_h, :, 128 * t : 128 * (t + 1)] = tile
 
     def self_copy(step):
@@ -326,7 +329,7 @@
     mixed_copy = pltpu.make_async_copy(mixed_v.at[:, my_rows(my_h)], mixed_out, loc_sem.at[0])
     mixed_copy.start()
 
-    queries = dot(x0[...], cproj_v[0]) * HEAD ** (-0.5)
+    queries = dot_nt(x0[...], cproj_v[0]) * HEAD ** (-0.5)
     q_tiles = pair_tiles(queries, None)
     for parity in range(2):
         for h in range(HEADS):
@@ -369,11 +372,10 @@
             device_id_type=MESH,
         )
 
-    def slot_contexts(j, parity):
+    def slot_tiles(j, parity):
         image = bits[j]
         return [
-            head_context(qbuf[parity, image, h], recvbuf[j, :, 128 * h : 128 * (h + 1)])
-            for h in range(HEADS)
+            (qbuf[parity, image, h], recvbuf[j, :, 128 * h : 128 * (h + 1)]) for h in range(HEADS)
         ]
 
     def finish_pair(pair, even, odd):
@@ -386,13 +388,12 @@
     @pl.loop(0, NEAR)
     def _(pair):
         kv_arrival(2 * pair, pair + 1).wait_recv()
-        even = slot_contexts(2 * pair, 0)
         kv_arrival(2 * pair + 1, -(pair + 1)).wait_recv()
-        odd = slot_contexts(2 * pair + 1, 1)
-        finish_pair(pair, even, odd)
+        contexts = head_contexts(slot_tiles(2 * pair, 0) + slot_tiles(2 * pair + 1, 1))
+        finish_pair(pair, contexts[:HEADS], contexts[HEADS:])
 
     kv_arrival(SLOTS - 1, 32).wait_recv()
-    finish_pair(PAIRS - 1, slot_contexts(SLOTS - 1, 0), None)
+    finish_pair(PAIRS - 1, head_contexts(slot_tiles(SLOTS - 1, 0)), None)
 
     for step in range(1, HELPERS):
         weight_arrival(1, step).wait_recv()
@@ -423,7 +424,7 @@
 
 
 def place_kernel(
-    part, ctx_hbm, w_hbm, mixed, out, ctx, w, terms, result, blank, ctx_sem, w_sem, out_sem
+    part, ctx_hbm, w_hbm, mixed, out, ctx, w, result, blank, places, ctx_sem, w_sem, out_sem, blank_sem
 ):
     me = lax.axis_index("owner")
     load_w = pltpu.make_async_copy(w_hbm, w.at[:, pl.ds(PAD, COLS)], w_sem)
@@ -433,20 +434,9 @@
     w[:, 0:PAD] = jnp.zeros((HELPERS, PAD, D), BF16)
     w[:, PAD + COLS :] = jnp.zeros((HELPERS, PAD, D), BF16)
     blank[...] = jnp.zeros((ROWS, D), BF16)
-    load_w.wait()
-    load_ctx.wait()
-    for parity in range(2):
-        total = None
-        for h in range(HELPERS):
-            if parity == 0:
-                term = dot(ctx[h, :, :, 0:256].reshape(PAIRS * ROWS, 256), w[h, PAD:])
-            else:
-                term = dot(ctx[h, :, :, 128:384].reshape(PAIRS * ROWS, 256), w[h, 0 : PAD + COLS])
-            total = term if total is None else total + term
-        terms[parity] = total.reshape(PAIRS, ROWS, D)
-
-    def out_copy(source, image, slot):
-        return pltpu.make_async_copy(source, out.at[image, slot], out_sem.at[image, slot])
+
+    def blank_copy(image, slot):
+        return pltpu.make_async_copy(blank, out.at[image, slot], blank_sem.at[image, slot])
 
     for image in range(IMAGES):
 
@@ -454,26 +444,59 @@
         def _(slot):
             p = part[image, slot]
             offset = (lax.div(jnp.maximum(p, 0), 2) - me + OWNERS) % OWNERS
-            far = offset == 32
             back = offset > 32
-            pair = jnp.where(far, PAIRS - 1, jnp.where(back, OWNERS - offset, offset) - 1)
-            pair = jnp.clip(pair, 0, PAIRS - 1)
-            parity = jnp.where(back, 1, 0)
+            near = jnp.where(back, 2 * (OWNERS - offset) - 1, 2 * offset - 2)
+            index = jnp.clip(jnp.where(offset == 32, SLOTS - 1, near), 0, SLOTS - 1)
 
             @pl.when(p >= 0)
             def _():
-                result[image, slot] = (terms[parity, pair] + mixed[image]).astype(BF16)
-                out_copy(result.at[image, slot], image, slot).start()
+                places[index] = image * SLOTS + slot
 
             @pl.when(p < 0)
             def _():
-                out_copy(blank, image, slot).start()
+                blank_copy(image, slot).start()
+
+    load_w.wait()
+    load_ctx.wait()
+
+    def out_copy(index):
+        place = places[index]
+        return pltpu.make_async_copy(
+            result.at[index],
+            out.at[lax.div(place, SLOTS), lax.rem(place, SLOTS)],
+            out_sem.at[index],
+        )
+
+    for first, count in ((0, 6), (6, 5)):
+        for parity in range(2):
+            start, weight_rows = (0, slice(PAD, None)) if parity == 0 else (128, slice(0, 256))
+            lhs = jnp.concatenate(
+                [
+                    ctx[h, first : first + count, :, start : start + 256].reshape(count * ROWS, 256)
+                    for h in range(HELPERS)
+                ],
+                axis=1,
+            )
+            rhs = jnp.concatenate([w[h, weight_rows] for h in range(HELPERS)], axis=0)
+            terms = dot(lhs, rhs)
+            for n in range(count):
+                index = 2 * (first + n) + parity
+                if index < SLOTS:
+                    image = lax.div(places[index], SLOTS)
+                    result[index] = (terms[ROWS * n : ROWS * (n + 1)] + mixed[image]).astype(BF16)
+                    out_copy(index).start()
+
+    @pl.loop(0, SLOTS)
+    def _(index):
+        out_copy(index).wait()
 
     for image in range(IMAGES):
 
         @pl.loop(0, SLOTS)
         def _(slot):
-            out_copy(blank, image, slot).wait()
+            @pl.when(part[image, slot] < 0)
+            def _():
+                blank_copy(image, slot).wait()
 
 
 def local(states, partners, self_proj, self_out, cross_proj, cross_out, gains):
@@ -492,8 +515,8 @@
         out_specs=(any_spec, any_spec, any_spec),
         scratch_shapes=[
             pltpu.VMEM((IMAGES, PATCHES, D), BF16),
-            pltpu.VMEM((3, D, COLS), BF16),
-            pltpu.VMEM((3, D, COLS), BF16),
+            pltpu.VMEM((3, COLS, D), BF16),
+            pltpu.VMEM((3, COLS, D), BF16),
             pltpu.VMEM((HELPERS, COLS + 2 * PAD, D), BF16),
             pltpu.VMEM((IMAGES * PATCHES, D), BF16),
             pltpu.VMEM((IMAGES * PATCHES, D), BF16),
@@ -523,7 +546,15 @@
             collective_id=0, has_side_effects=True, vmem_limit_bytes=VMEM_LIMIT
         ),
         name="exchange",
-    )(partners, states, self_proj, self_out, cross_proj, cross_out, gains)
+    )(
+        partners,
+        states,
+        jnp.swapaxes(self_proj, 1, 2),
+        self_out,
+        jnp.swapaxes(cross_proj, 1, 2),
+        cross_out,
+        gains,
+    )
     return pl.pallas_call(
         place_kernel,
         out_shape=jax.ShapeDtypeStruct((IMAGES, SLOTS, ROWS, D), BF16),
@@ -532,11 +563,12 @@
         scratch_shapes=[
             pltpu.VMEM((HELPERS, PAIRS, ROWS, LANES), BF16),
             pltpu.VMEM((HELPERS, COLS + 2 * PAD, D), BF16),
-            pltpu.VMEM((2, PAIRS, ROWS, D), F32),
-            pltpu.VMEM((IMAGES, SLOTS, ROWS, D), BF16),
+            pltpu.VMEM((SLOTS, ROWS, D), BF16),
             pltpu.VMEM((ROWS, D), BF16),
+            pltpu.SMEM((SLOTS,), jnp.int32),
             dma,
             dma,
+            dma((SLOTS,)),
             dma((IMAGES, SLOTS)),
         ],
         compiler_params=pltpu.CompilerParams(vmem_limit_bytes=VMEM_LIMIT),

time: 65.4 us -> 60.1 us (0.919)
  local copies, waits for them, and re-layouts: 3.82 us -> 0 us
  Pallas kernels: 61.4 us -> 59.9 us
    unnamed x4 -> x0, local copies, waits for them, and re-layouts: 3.82 us -> none
    pallas_call x1, Pallas kernels: 55.3 us -> 54.1 us  [local(): pl.pallas_call(exchange_kernel, out_shape=(jax.ShapeDtypeStruct((HELPERS,...]
where the time goes in v2:
time: 60.1 us; the launch traced here: 59.9 us
  Pallas kernels  59.9 us (100%)
    pallas_call x1, Pallas kernels, local(): pl.pallas_call(exchange_kernel, out_shape=(jax.ShapeDtypeStruct((HELPERS,...  54.1 us
    pallas_call x1, Pallas kernels, local(): pl.pallas_call(place_kernel, out_shape=jax.ShapeDtypeStruct((IMAGES, SLOT...  5.7 us

profile of v2, /device:TPU:1, one launch (start us, length us, event | category | flops | bytes accessed | tf_op | source)
XLA Modules:
  0.0 59.9 jit_solution(10703652906764320815)
XLA Ops:
  0.0 54.1 %exchange.1 = (bf16[4,11,32,384]{3,2,1,0:T(8,128)(2,1)}, bf16[4,192,768]{2,1,0:T(8,128)(2,1)}, f32[2,32,768]{2,1,0:T(8,128)}) custom-call(s32[2,21]{1,0:T(2,128)} %part.3, bf16[2,128,768]{2,1,0:T(8,128)(2,1)} %states_hbm.1, bf16[3,192,768]{2,1,0:T(8,128)(2,1)} %bitcast.2, bf16[192,768]{1,0:T(8,128)(2,1)} %sout_hbm.1, bf16[3,192,768]{2,1,0:T(8,128)(2,1)} %bitcast.3, ...), custom_call_target="tpu_custom_call" | custom-call | tf_op jit(solution)/shard_map/exchange/pallas_call | solution.py:507
  54.2 5.7 %place.1 = bf16[2,21,32,768]{3,2,1,0:T(8,128)(2,1)} custom-call(s32[2,21]{1,0:T(2,128)} %part.3, bf16[4,11,32,384]{3,2,1,0:T(8,128)(2,1)} %get-tuple-element.8.ctx_hbm, bf16[4,192,768]{2,1,0:T(8,128)(2,1)} %get-tuple-element.9.w_hbm, f32[2,32,768]{2,1,0:T(8,128)} %get-tuple-element.10.mixed), custom_call_target="tpu_custom_call" | custom-call | tf_op jit(solution)/shard_map/place/pallas_call | solution.py:558

commit v3 on v2

v3 whole, which is shorter than its diff:
```python
import functools

import jax
import jax.numpy as jnp
from jax import lax
from jax.experimental import pallas as pl
from jax.experimental.pallas import tpu as pltpu
from jax.sharding import PartitionSpec as P

MESH = pl.DeviceIdType.MESH
BF16 = jnp.bfloat16
F32 = jnp.float32

OWNERS = 64
HELPERS = 4
IMAGES = 2
PATCHES = 128
ROWS = PATCHES // HELPERS
D = 768
HEAD = 64
HEADS = 3
COLS = HEADS * HEAD
SLOTS = 21
X, Z = 4, 8
PAIRS = 11
ACROSS = 80
WPIECE = COLS // X
LANES = 2 * COLS
PAD = 64
COPIES = 56
VMEM_LIMIT = 56 * 1024 * 1024


def dot(a, b):
    return jnp.dot(a, b, preferred_element_type=F32)


def dot_nt(a, b):
    return lax.dot_general(a, b, (((1,), (1,)), ((), ())), preferred_element_type=F32)


def pair_tiles(first, second):
    zero = jnp.zeros((first.shape[0], HEAD), F32)
    f = [first[:, HEAD * h : HEAD * (h + 1)] for h in range(HEADS)]
    s = [zero] * HEADS if second is None else [second[:, HEAD * h : HEAD * (h + 1)] for h in range(HEADS)]
    tiles = []
    for parity in range(2):
        row = []
        for h in range(HEADS):
            ordered = (s[h], f[h]) if (h + parity) % 2 == 0 else (f[h], s[h])
            row.append(jnp.concatenate(ordered, axis=1).astype(BF16))
        tiles.append(row)
    return tiles


def head_contexts(tiles):
    scores = [dot_nt(q, kv) for q, kv in tiles]
    weights = [jnp.exp(s - jnp.max(s, axis=1, keepdims=True)) for s in scores]
    totals = [jnp.sum(w, axis=1, keepdims=True) for w in weights]
    return [
        dot(w.astype(BF16), kv) * (1.0 / t) for w, t, (_, kv) in zip(weights, totals, tiles)
    ]


def join_contexts(even, odd):
    low = lax.broadcasted_iota(jnp.int32, (PATCHES, 2 * HEAD), 1) < HEAD
    if odd is None:
        odd = [even[0], even[1], even[0]]
    return (
        jnp.where(low, even[0], even[1]).astype(BF16),
        jnp.where(low, even[2], odd[0]).astype(BF16),
        jnp.where(low, odd[1], odd[2]).astype(BF16),
    )


def slot_owner(pair, parity, core):
    group = pair // 2
    size = jnp.where(group == 0, 4, jnp.where(group == 1, 1, jnp.where(group == 2, 3, 2)))
    both = 10 * core - 5
    single = jnp.where(parity == 0, 5 * (1 - core), -5 * core)
    offset = jnp.where(pair < 8, size * (1 - 2 * (pair % 2)), jnp.where(pair == 8, both, single))
    return offset, (parity + core) % 2


def exchange_kernel(
    part,
    states_hbm,
    sproj_hbm,
    sout_hbm,
    cproj_hbm,
    cout_hbm,
    gains,
    ctx_out,
    w_out,
    mixed_out,
    states_v,
    sproj_v,
    cproj_v,
    sw,
    x0,
    x2,
    kvbuf,
    far_send,
    far_recv,
    gathered,
    sums,
    sums_recv,
    mixed_v,
    normed,
    qbuf,
    ctxbuf,
    own_bits,
    partner_bits,
    in_sem,
    loc_sem,
    own_sem,
    send_sem,
    recv_sem,
    c_send,
    c_recv,
):
    me = lax.axis_index("owner")
    my_h = lax.axis_index("helper")
    core = me % 2
    chip = me // 2
    my_x = chip % X
    my_z = chip // X

    def chip_at(dz, dx):
        return (((my_z + dz + Z) % Z) * 2 * X + ((my_x + dx + X) % X) * 2 + core, my_h)

    def helper_at(step):
        return (me, (my_h + step) % HELPERS)

    sibling = (me + 1 - 2 * core, my_h)
    north, south, east, west = chip_at(1, 0), chip_at(-1, 0), chip_at(0, 1), chip_at(0, -1)
    far = chip_at(4, 0)
    greeted = [north, south, east, west, chip_at(0, 2), far, sibling]
    greeted += [helper_at(step) for step in range(1, HELPERS)]
    barrier = pltpu.get_barrier_semaphore()
    for device in greeted:
        pl.semaphore_signal(barrier, inc=1, device_id=device, device_id_type=MESH)

    loads = [
        pltpu.make_async_copy(states_hbm, states_v, in_sem.at[0]),
        pltpu.make_async_copy(cproj_hbm, cproj_v, in_sem.at[1]),
        pltpu.make_async_copy(sproj_hbm, sproj_v, in_sem.at[2]),
        pltpu.make_async_copy(sout_hbm, sw.at[pl.ds(PAD, COLS)], in_sem.at[3]),
        pltpu.make_async_copy(cout_hbm, w_out.at[0], in_sem.at[4]),
    ]
    for load in loads:
        load.start()

    copies = {}

    def send(name, source, landing, device, when=None, seen=None):
        number = len(copies)

        def describe(place):
            return pltpu.make_async_remote_copy(
                src_ref=source,
                dst_ref=place,
                send_sem=send_sem.at[number],
                recv_sem=recv_sem.at[number],
                device_id=device,
                device_id_type=MESH,
            )

        copies[name] = (functools.partial(describe, landing), functools.partial(describe, seen or landing), when)
        if when is None:
            describe(landing).start()
        else:
            pl.when(when)(lambda: describe(landing).start())

    def arrived(*names):
        for name in names:
            _, seen, when = copies[name]
            if when is None:
                seen().wait_recv()
            else:
                pl.when(when)(lambda: seen().wait_recv())

    mine, other = gathered.at[0], gathered.at[1]

    def share(row, col, when=None):
        send(f"s{row}{col}", mine.at[row, col], other.at[row, col], sibling, when)

    loads[0].wait()
    as_float = states_v[...].reshape(IMAGES * PATCHES, D).astype(F32)
    row_mean = jnp.mean(as_float, -1, keepdims=True)
    centred = as_float - row_mean
    row_var = jnp.mean(centred * centred, -1, keepdims=True)
    scaled = centred * lax.rsqrt(row_var + 1e-05)
    x2[...] = (scaled * gains[2:3, :]).astype(BF16)
    x0[...] = (scaled * gains[0:1, :]).astype(BF16)

    loads[1].wait()
    key_rows = dot_nt(x2[...], cproj_v[1])
    value_rows = dot_nt(x2[...], cproj_v[2])
    tiles = pair_tiles(key_rows, value_rows)
    for parity in range(2):
        for h in range(HEADS):
            for image in range(IMAGES):
                kvbuf[parity, image, :, 128 * h : 128 * (h + 1)] = tiles[parity][h][
                    PATCHES * image : PATCHES * (image + 1)
                ]

    opposite = 2 * ((me + OWNERS // 2) % OWNERS)
    far_bit = jnp.int32(0)
    for s in range(SLOTS):
        p = part[1, s]
        far_bit = jnp.where(jnp.logical_and(p >= opposite, p <= opposite + 1), 1, far_bit)
    far_send[...] = kvbuf[0, far_bit]

    pl.semaphore_wait(barrier, len(greeted))

    own = kvbuf.at[core]
    send("x+0", own.at[0], mine.at[2, 3, 0], east)
    send("x-1", own.at[1], mine.at[2, 1, 1], west)
    send("z+", own, mine.at[1, 0], north)
    send("z-", own, mine.at[3, 0], south)
    send("x+1", own.at[1], mine.at[2, 3, 1], east)
    send("x-0", own.at[0], mine.at[2, 1, 0], west)
    send("s20", own, other.at[2, 0], sibling)

    def weight_piece(x):
        return pl.ds(pl.multiple_of(x * WPIECE, 16), WPIECE)

    def weight_half(c):
        return pl.ds(pl.multiple_of(c * (D // 2), 128), D // 2)

    for step in range(1, HELPERS):
        send(
            f"w{step}",
            cout_hbm.at[weight_piece(my_x), weight_half(core)],
            w_out.at[HELPERS - step, weight_piece(my_x), weight_half(core)],
            helper_at(step),
        )

    sw[0:PAD] = jnp.zeros((PAD, D), BF16)
    sw[PAD + COLS :] = jnp.zeros((PAD, D), BF16)
    loads[2].wait()
    sq = dot_nt(x0[...], sproj_v[0]) * HEAD ** (-0.5)
    sk = dot_nt(x0[...], sproj_v[1])
    sv = dot_nt(x0[...], sproj_v[2])
    q_tiles = pair_tiles(sq, None)
    kv_tiles = pair_tiles(sk, sv)
    pieces = [slice(PATCHES * image, PATCHES * (image + 1)) for image in range(IMAGES)]
    contexts = head_contexts(
        [
            (q_tiles[image][h][pieces[image]], kv_tiles[image][h][pieces[image]])
            for image in range(IMAGES)
            for h in range(HEADS)
        ]
    )
    joined = join_contexts(contexts[:HEADS], contexts[HEADS:])
    loads[3].wait()
    sums[0] = dot(jnp.concatenate(joined[0:2], axis=1), sw[PAD:]).astype(BF16)
    sums[1] = dot(jnp.concatenate(joined[1:3], axis=1), sw[0 : PAD + COLS]).astype(BF16)

    def rows_of(step):
        return pl.ds(pl.multiple_of(((my_h + step) % HELPERS) * ROWS, ROWS), ROWS)

    for step in range(1, HELPERS):
        send(f"p{step}", sums.at[:, rows_of(step)], sums_recv.at[step - 1], helper_at(step))

    over_x, over_z = pl.ds(0, ACROSS), pl.ds(ACROSS, PATCHES - ACROSS)
    arrived("x+0")
    send("x++", mine.at[2, 3, 0], mine.at[2, 2, 0], east)
    arrived("x-1")
    send("x--", mine.at[2, 1, 1], mine.at[2, 2, 1], west)
    arrived("x+1")
    send("x+z+", mine.at[2, 3, :, over_z], mine.at[1, 3, :, over_z], north)
    send("x+z-", mine.at[2, 3, :, over_z], mine.at[3, 3, :, over_z], south)
    arrived("x-0")
    send("x-z+", mine.at[2, 1, :, over_z], mine.at[1, 1, :, over_z], north)
    send("x-z-", mine.at[2, 1, :, over_z], mine.at[3, 1, :, over_z], south)
    arrived("z+")
    send("z+x+", mine.at[1, 0, :, over_x], mine.at[1, 3, :, over_x], east)
    send("z+x-", mine.at[1, 0, :, over_x], mine.at[1, 1, :, over_x], west)
    arrived("z-")
    send("z-x+", mine.at[3, 0, :, over_x], mine.at[3, 3, :, over_x], east)
    send("z-x-", mine.at[3, 0, :, over_x], mine.at[3, 1, :, over_x], west)
    send("far", far_send, far_recv, far)
    share(2, 3)
    share(2, 1)
    share(1, 0)
    share(3, 0)

    arrived("p1", "p2", "p3")
    mixed_v[...] = (
        states_v[:, rows_of(0)].astype(F32)
        + sums[:, rows_of(0)].astype(F32)
        + sums_recv[0].astype(F32)
        + sums_recv[1].astype(F32)
        + sums_recv[2].astype(F32)
    )
    mixed = mixed_v[...]
    row_mean = jnp.mean(mixed, -1, keepdims=True)
    centred = mixed - row_mean
    row_var = jnp.mean(centred * centred, -1, keepdims=True)
    normed[0] = (centred * lax.rsqrt(row_var + 1e-05) * gains[1:2, :].reshape(1, 1, D)).astype(BF16)
    for step in range(1, HELPERS):
        send(f"n{step}", normed.at[0], normed.at[HELPERS - step], helper_at(step))
    mixed_copy = pltpu.make_async_copy(mixed_v, mixed_out, loc_sem.at[0])
    mixed_copy.start()

    arrived("w1", "w2", "w3")
    for step in (1, 3, 2):
        send(
            f"wx{step}",
            w_out.at[pl.ds(1, 3), weight_piece(my_x), weight_half(core)],
            w_out.at[pl.ds(1, 3), weight_piece(my_x), weight_half(core)],
            chip_at(0, step),
            seen=w_out.at[pl.ds(1, 3), weight_piece((my_x + X - step) % X), weight_half(core)],
        )

    @pl.loop(0, SLOTS)
    def _(m):
        offset, layer = slot_owner(m // 2, m % 2, core)
        target = 2 * ((chip + offset + OWNERS // 2) % (OWNERS // 2)) + (layer + core) % 2
        target = 2 * jnp.where(m == SLOTS - 1, (me + OWNERS // 2) % OWNERS, target)
        code = jnp.int32(0)
        for image in range(IMAGES):
            for s in range(SLOTS):
                past = part[image, s] - target
                hit = jnp.logical_and(past >= 0, past <= 1)
                code = jnp.where(hit, 2 * image + past, code)
        own_bits[m] = code // 2
        partner_bits[m] = code % 2

    arrived("x--", "x++")
    send("x2z+", mine.at[2, 2, :, over_z], mine.at[1, 2, :, over_z], north)
    send("x2z-", mine.at[2, 2, :, over_z], mine.at[3, 2, :, over_z], south)
    share(2, 2)
    arrived("z+x+")
    send("z+x++", mine.at[1, 3, :, over_x], mine.at[1, 2, :, over_x], east)
    arrived("z-x-")
    send("z-x--", mine.at[3, 1, :, over_x], mine.at[3, 2, :, over_x], west)
    first_x, last_x = my_x == 0, my_x == X - 1
    arrived("x+z+")
    send("c0", mine.at[1, 3], mine.at[0, 3], north, first_x)
    share(1, 3)
    arrived("x-z-")
    send("c3", mine.at[3, 1], mine.at[4, 1], south, last_x)
    share(3, 1)

    arrived("n1", "n2", "n3")
    queries = dot_nt(normed[...].reshape(IMAGES * PATCHES, D), cproj_v[0]) * HEAD ** (-0.5)
    q_tiles = pair_tiles(queries, None)
    for parity in range(2):
        for h in range(HEADS):
            for step in range(HELPERS):
                for image in range(IMAGES):
                    start = ROWS * (IMAGES * step + image)
                    qbuf[parity, image, h, rows_of(step)] = q_tiles[parity][h][start : start + ROWS]

    def context_copy(pair, step):
        return pltpu.make_async_remote_copy(
            src_ref=ctxbuf.at[pair, rows_of(step)],
            dst_ref=ctx_out.at[HELPERS - step, pair],
            send_sem=c_send.at[pair, step - 1],
            recv_sem=c_recv.at[pair, step - 1],
            device_id=helper_at(step),
            device_id_type=MESH,
        )

    def own_copy(pair):
        return pltpu.make_async_copy(
            ctxbuf.at[pair, rows_of(0)], ctx_out.at[0, pair], own_sem.at[pair]
        )

    def slot_tiles(pair, parity):
        m = 2 * pair + parity
        offset, layer = slot_owner(pair, parity, core)
        col = (offset + 2 * X) % X
        row = (my_x + offset + 2 * X) // X
        image, which = own_bits[m], partner_bits[m]
        kv = jnp.where(
            which == 1, gathered[layer, row, col, 1], gathered[layer, row, col, 0]
        )
        return [
            (qbuf[parity, image, h], kv[:, 128 * h : 128 * (h + 1)]) for h in range(HEADS)
        ]

    def finish_pair(pair, even, odd):
        for t, tile in enumerate(join_contexts(even, odd)):
            ctxbuf[pair, :, 128 * t : 128 * (t + 1)] = tile
        for step in (2, 1, 3):
            context_copy(pair, step).start()
        own_copy(pair).start()

    def work_pairs(first, last):
        @pl.loop(first, last)
        def _(pair):
            contexts = head_contexts(slot_tiles(pair, 0) + slot_tiles(pair, 1))
            finish_pair(pair, contexts[:HEADS], contexts[HEADS:])

    arrived("s10", "s30")
    work_pairs(0, 2)
    arrived("z+x-", "x-z+")
    share(1, 1)
    arrived("z-x+", "x+z-")
    share(3, 3)
    arrived("s23", "s21", "s13", "s31", "s11", "s33")
    work_pairs(2, 6)
    arrived("z+x++", "x2z+")
    share(1, 2)
    arrived("z-x--", "x2z-")
    share(3, 2)
    arrived("wx1", "wx2", "wx3")
    send(
        "ws",
        w_out.at[pl.ds(1, 3), :, weight_half(core)],
        w_out.at[pl.ds(1, 3), :, weight_half(core)],
        sibling,
        seen=w_out.at[pl.ds(1, 3), :, weight_half(1 - core)],
    )
    arrived("s22", "s12", "s32")
    work_pairs(6, 8)
    arrived("c0", "c3")
    share(0, 3, first_x)
    share(4, 1, last_x)
    arrived("s20", "s03", "s41")
    work_pairs(8, 10)
    arrived("far")
    far_tiles = [
        (qbuf[0, own_bits[SLOTS - 1], h], far_recv[:, 128 * h : 128 * (h + 1)]) for h in range(HEADS)
    ]
    finish_pair(PAIRS - 1, head_contexts(far_tiles), None)

    arrived("ws")
    loads[4].wait()
    mixed_copy.wait()
    for sent, _, when in copies.values():
        if when is None:
            sent().wait_send()
        else:
            pl.when(when)(lambda: sent().wait_send())

    @pl.loop(0, PAIRS)
    def _(pair):
        for step in range(1, HELPERS):
            context_copy(pair, step).wait()
        own_copy(pair).wait()


def place_kernel(
    part, ctx_hbm, w_hbm, mixed, out, ctx, w, result, blank, places, ctx_sem, w_sem, out_sem, blank_sem
):
    me = lax.axis_index("owner")
    load_w = pltpu.make_async_copy(w_hbm, w.at[:, pl.ds(PAD, COLS)], w_sem)
    load_ctx = pltpu.make_async_copy(ctx_hbm, ctx, ctx_sem)
    load_w.start()
    load_ctx.start()
    w[:, 0:PAD] = jnp.zeros((HELPERS, PAD, D), BF16)
    w[:, PAD + COLS :] = jnp.zeros((HELPERS, PAD, D), BF16)
    blank[...] = jnp.zeros((ROWS, D), BF16)

    def blank_copy(image, slot):
        return pltpu.make_async_copy(blank, out.at[image, slot], blank_sem.at[image, slot])

    for image in range(IMAGES):

        @pl.loop(0, SLOTS)
        def _(slot):
            p = part[image, slot]
            owner = lax.div(jnp.maximum(p, 0), 2)
            parity = owner % 2
            chips = OWNERS // 2
            offset = (owner // 2 - me // 2 + chips + chips // 2) % chips - chips // 2
            size = jnp.abs(offset)
            group = jnp.where(size == 4, 0, jnp.where(size == 1, 1, jnp.where(size == 3, 2, 3)))
            pair = 2 * group + jnp.where(offset < 0, 1, 0)
            pair = jnp.where(size == 5, jnp.where(offset == 10 * (me % 2) - 5, 8, 9), pair)
            pair = jnp.where(size == 0, 9, pair)
            index = jnp.where(size == chips // 2, SLOTS - 1, 2 * pair + parity)
            index = jnp.clip(index, 0, SLOTS - 1)

            @pl.when(p >= 0)
            def _():
                places[index] = image * SLOTS + slot

            @pl.when(p < 0)
            def _():
                blank_copy(image, slot).start()

    load_w.wait()
    load_ctx.wait()

    def out_copy(index):
        place = places[index]
        return pltpu.make_async_copy(
            result.at[index],
            out.at[lax.div(place, SLOTS), lax.rem(place, SLOTS)],
            out_sem.at[index],
        )

    for first, count in ((0, 6), (6, 5)):
        for parity in range(2):
            start, weight_rows = (0, slice(PAD, None)) if parity == 0 else (128, slice(0, 256))
            lhs = jnp.concatenate(
                [
                    ctx[h, first : first + count, :, start : start + 256].reshape(count * ROWS, 256)
                    for h in range(HELPERS)
                ],
                axis=1,
            )
            rhs = jnp.concatenate([w[h, weight_rows] for h in range(HELPERS)], axis=0)
            terms = dot(lhs, rhs)
            for n in range(count):
                index = 2 * (first + n) + parity
                if index < SLOTS:
                    image = lax.div(places[index], SLOTS)
                    result[index] = (terms[ROWS * n : ROWS * (n + 1)] + mixed[image]).astype(BF16)
                    out_copy(index).start()

    @pl.loop(0, SLOTS)
    def _(index):
        out_copy(index).wait()

    for image in range(IMAGES):

        @pl.loop(0, SLOTS)
        def _(slot):
            @pl.when(part[image, slot] < 0)
            def _():
                blank_copy(image, slot).wait()


def local(states, partners, self_proj, self_out, cross_proj, cross_out, gains):
    any_spec = pl.BlockSpec(memory_space=pl.ANY)
    smem = pl.BlockSpec(memory_space=pltpu.SMEM)
    vmem = pl.BlockSpec(memory_space=pltpu.VMEM)
    dma = pltpu.SemaphoreType.DMA
    ctx, weight, mixed = pl.pallas_call(
        exchange_kernel,
        out_shape=(
            jax.ShapeDtypeStruct((HELPERS, PAIRS, ROWS, LANES), BF16),
            jax.ShapeDtypeStruct((HELPERS, COLS, D), BF16),
            jax.ShapeDtypeStruct((IMAGES, ROWS, D), F32),
        ),
        in_specs=[smem, any_spec, any_spec, any_spec, any_spec, any_spec, vmem],
        out_specs=(any_spec, any_spec, any_spec),
        scratch_shapes=[
            pltpu.VMEM((IMAGES, PATCHES, D), BF16),
            pltpu.VMEM((3, COLS, D), BF16),
            pltpu.VMEM((3, COLS, D), BF16),
            pltpu.VMEM((COLS + 2 * PAD, D), BF16),
            pltpu.VMEM((IMAGES * PATCHES, D), BF16),
            pltpu.VMEM((IMAGES * PATCHES, D), BF16),
            pltpu.VMEM((2, IMAGES, PATCHES, LANES), BF16),
            pltpu.VMEM((PATCHES, LANES), BF16),
            pltpu.VMEM((PATCHES, LANES), BF16),
            pltpu.VMEM((2, 5, X, IMAGES, PATCHES, LANES), BF16),
            pltpu.VMEM((IMAGES, PATCHES, D), BF16),
            pltpu.VMEM((HELPERS - 1, IMAGES, ROWS, D), BF16),
            pltpu.VMEM((IMAGES, ROWS, D), F32),
            pltpu.VMEM((HELPERS, IMAGES, ROWS, D), BF16),
            pltpu.VMEM((2, IMAGES, HEADS, PATCHES, 2 * HEAD), BF16),
            pltpu.VMEM((PAIRS, PATCHES, LANES), BF16),
            pltpu.SMEM((SLOTS,), jnp.int32),
            pltpu.SMEM((SLOTS,), jnp.int32),
            dma((5,)),
            dma((1,)),
            dma((PAIRS,)),
            dma((COPIES,)),
            dma((COPIES,)),
            dma((PAIRS, 3)),
            dma((PAIRS, 3)),
        ],
        compiler_params=pltpu.CompilerParams(
            collective_id=0, has_side_effects=True, vmem_limit_bytes=VMEM_LIMIT
        ),
        name="exchange",
    )(
        partners,
        states,
        jnp.swapaxes(self_proj, 1, 2),
        self_out,
        jnp.swapaxes(cross_proj, 1, 2),
        cross_out,
        gains,
    )
    return pl.pallas_call(
        place_kernel,
        out_shape=jax.ShapeDtypeStruct((IMAGES, SLOTS, ROWS, D), BF16),
        in_specs=[smem, any_spec, any_spec, vmem],
        out_specs=any_spec,
        scratch_shapes=[
            pltpu.VMEM((HELPERS, PAIRS, ROWS, LANES), BF16),
            pltpu.VMEM((HELPERS, COLS + 2 * PAD, D), BF16),
            pltpu.VMEM((SLOTS, ROWS, D), BF16),
            pltpu.VMEM((ROWS, D), BF16),
            pltpu.SMEM((SLOTS,), jnp.int32),
            dma,
            dma,
            dma((SLOTS,)),
            dma((IMAGES, SLOTS)),
        ],
        compiler_params=pltpu.CompilerParams(vmem_limit_bytes=VMEM_LIMIT),
        name="place",
    )(partners, ctx, weight, mixed)


def solution(mesh):
    return jax.shard_map(
        local,
        mesh=mesh,
        in_specs=(
            P("owner", None, None),
            P("owner", None),
            P(None, None, "helper"),
            P("helper", None),
            P(None, None, "helper"),
            P("helper", None),
            P(),
        ),
        out_specs=P("owner", None, "helper", None),
        check_vma=False,
    )
```

time: 60.1 us -> 48.5 us (0.81)
  Pallas kernels: 59.9 us -> 47.9 us
    pallas_call x1, Pallas kernels: 54.1 us -> 42.3 us  [local(): pl.pallas_call(exchange_kernel, out_shape=(jax.ShapeDtypeStruct((HELPERS,...]
where the time goes in v3:
time: 48.5 us; the launch traced here: 47.9 us
  Pallas kernels  47.9 us (99%)
    pallas_call x1, Pallas kernels, local(): pl.pallas_call(exchange_kernel, out_shape=(jax.ShapeDtypeStruct((HELPERS,...  42.3 us
    pallas_call x1, Pallas kernels, local(): pl.pallas_call(place_kernel, out_shape=jax.ShapeDtypeStruct((IMAGES, SLOT...  5.56 us

profile of v3, /device:TPU:1, one launch (start us, length us, event | category | flops | bytes accessed | tf_op | source)
XLA Modules:
  0.0 47.9 jit_solution(2058496724658499685)
XLA Ops:
  0.0 42.3 %exchange.1 = (bf16[4,11,32,384]{3,2,1,0:T(8,128)(2,1)}, bf16[4,192,768]{2,1,0:T(8,128)(2,1)}, f32[2,32,768]{2,1,0:T(8,128)}) custom-call(s32[2,21]{1,0:T(2,128)} %part.3, bf16[2,128,768]{2,1,0:T(8,128)(2,1)} %states_hbm.1, bf16[3,192,768]{2,1,0:T(8,128)(2,1)} %bitcast.2, bf16[192,768]{1,0:T(8,128)(2,1)} %sout_hbm.1, bf16[3,192,768]{2,1,0:T(8,128)(2,1)} %bitcast.3, ...), custom_call_target="tpu_custom_call" | custom-call | tf_op jit(solution)/shard_map/exchange/pallas_call | solution.py:536
  42.3 5.6 %place.1 = bf16[2,21,32,768]{3,2,1,0:T(8,128)(2,1)} custom-call(s32[2,21]{1,0:T(2,128)} %part.3, bf16[4,11,32,384]{3,2,1,0:T(8,128)(2,1)} %get-tuple-element.8.ctx_hbm, bf16[4,192,768]{2,1,0:T(8,128)(2,1)} %get-tuple-element.9.w_hbm, f32[2,32,768]{2,1,0:T(8,128)} %get-tuple-element.10.mixed), custom_call_target="tpu_custom_call" | custom-call | tf_op jit(solution)/shard_map/place/pallas_call | solution.py:585

commit v4 on v3

--- a/solution.py
+++ b/solution.py
@@ -27,7 +27,7 @@
 WPIECE = COLS // X
 LANES = 2 * COLS
 PAD = 64
-COPIES = 56
+COPIES = 64
 VMEM_LIMIT = 56 * 1024 * 1024
 
 
@@ -82,6 +82,32 @@
     return offset, (parity + core) % 2
 
 
+def pair_at(n, x, core):
+    first, last = x == 0, x == X - 1
+
+    def pick(at_first, inside, at_last):
+        return jnp.where(first, at_first, jnp.where(last, at_last, inside))
+
+    low = x < X // 2
+    eighth = pick(9 - core, 8, 8 + core)
+    choices = [
+        0,
+        1,
+        pick(2, 2, 3),
+        pick(4, 3, 5),
+        pick(3, 4, 2),
+        pick(5, 5, 4),
+        jnp.where(low, 6, 7),
+        eighth,
+        jnp.where(low, 7, 6),
+        17 - eighth,
+    ]
+    pair = jnp.int32(0)
+    for step, choice in enumerate(choices):
+        pair = jnp.where(n == step, choice, pair)
+    return pair
+
+
 def exchange_kernel(
     part,
     states_hbm,
@@ -90,9 +116,7 @@
     cproj_hbm,
     cout_hbm,
     gains,
-    ctx_out,
-    w_out,
-    mixed_out,
+    y_out,
     states_v,
     sproj_v,
     cproj_v,
@@ -109,11 +133,14 @@
     normed,
     qbuf,
     ctxbuf,
+    ctx_recv,
+    w_all,
+    y,
     own_bits,
     partner_bits,
     in_sem,
-    loc_sem,
-    own_sem,
+    y_sem,
+    token_sem,
     send_sem,
     recv_sem,
     c_send,
@@ -135,7 +162,7 @@
     sibling = (me + 1 - 2 * core, my_h)
     north, south, east, west = chip_at(1, 0), chip_at(-1, 0), chip_at(0, 1), chip_at(0, -1)
     far = chip_at(4, 0)
-    greeted = [north, south, east, west, chip_at(0, 2), far, sibling]
+    greeted = [north, south, east, west, chip_at(0, 2), sibling]
     greeted += [helper_at(step) for step in range(1, HELPERS)]
     barrier = pltpu.get_barrier_semaphore()
     for device in greeted:
@@ -146,7 +173,7 @@
         pltpu.make_async_copy(cproj_hbm, cproj_v, in_sem.at[1]),
         pltpu.make_async_copy(sproj_hbm, sproj_v, in_sem.at[2]),
         pltpu.make_async_copy(sout_hbm, sw.at[pl.ds(PAD, COLS)], in_sem.at[3]),
-        pltpu.make_async_copy(cout_hbm, w_out.at[0], in_sem.at[4]),
+        pltpu.make_async_copy(cout_hbm, w_all.at[0, pl.ds(PAD, COLS)], in_sem.at[4]),
     ]
     for load in loads:
         load.start()
@@ -179,6 +206,13 @@
                 seen().wait_recv()
             else:
                 pl.when(when)(lambda: seen().wait_recv())
+
+    def token(n):
+        if n > 1:
+            pl.semaphore_wait(token_sem.at[n - 2], 2)
+        if n < 4:
+            for device in (north, south):
+                pl.semaphore_signal(token_sem.at[n - 1], inc=1, device_id=device, device_id_type=MESH)
 
     mine, other = gathered.at[0], gathered.at[1]
 
@@ -223,49 +257,61 @@
     send("x-0", own.at[0], mine.at[2, 1, 0], west)
     send("s20", own, other.at[2, 0], sibling)
 
+    token(1)
+
     def weight_piece(x):
         return pl.ds(pl.multiple_of(x * WPIECE, 16), WPIECE)
 
+    def weight_rows(x):
+        return pl.ds(pl.multiple_of(PAD + x * WPIECE, 16), WPIECE)
+
     def weight_half(c):
         return pl.ds(pl.multiple_of(c * (D // 2), 128), D // 2)
 
-    for step in range(1, HELPERS):
-        send(
-            f"w{step}",
-            cout_hbm.at[weight_piece(my_x), weight_half(core)],
-            w_out.at[HELPERS - step, weight_piece(my_x), weight_half(core)],
-            helper_at(step),
-        )
-
     sw[0:PAD] = jnp.zeros((PAD, D), BF16)
     sw[PAD + COLS :] = jnp.zeros((PAD, D), BF16)
+    w_all[:, 0:PAD] = jnp.zeros((HELPERS, PAD, D), BF16)
+    w_all[:, PAD + COLS :] = jnp.zeros((HELPERS, PAD, D), BF16)
     loads[2].wait()
     sq = dot_nt(x0[...], sproj_v[0]) * HEAD ** (-0.5)
     sk = dot_nt(x0[...], sproj_v[1])
     sv = dot_nt(x0[...], sproj_v[2])
     q_tiles = pair_tiles(sq, None)
     kv_tiles = pair_tiles(sk, sv)
-    pieces = [slice(PATCHES * image, PATCHES * (image + 1)) for image in range(IMAGES)]
-    contexts = head_contexts(
-        [
-            (q_tiles[image][h][pieces[image]], kv_tiles[image][h][pieces[image]])
-            for image in range(IMAGES)
-            for h in range(HEADS)
-        ]
-    )
-    joined = join_contexts(contexts[:HEADS], contexts[HEADS:])
-    loads[3].wait()
-    sums[0] = dot(jnp.concatenate(joined[0:2], axis=1), sw[PAD:]).astype(BF16)
-    sums[1] = dot(jnp.concatenate(joined[1:3], axis=1), sw[0 : PAD + COLS]).astype(BF16)
-
     def rows_of(step):
         return pl.ds(pl.multiple_of(((my_h + step) % HELPERS) * ROWS, ROWS), ROWS)
 
+    loads[3].wait()
+    for image in range(IMAGES):
+        piece = slice(PATCHES * image, PATCHES * (image + 1))
+        contexts = head_contexts(
+            [(q_tiles[image][h][piece], kv_tiles[image][h][piece]) for h in range(HEADS)]
+        )
+        if image == 0:
+            joined = join_contexts(contexts, None)[0:2]
+            sums[0] = dot(jnp.concatenate(joined, axis=1), sw[PAD:]).astype(BF16)
+        else:
+            joined = join_contexts([contexts[1], contexts[0], contexts[1]], contexts)[1:3]
+            sums[1] = dot(jnp.concatenate(joined, axis=1), sw[0 : PAD + COLS]).astype(BF16)
+        for step in range(1, HELPERS):
+            send(
+                f"p{step}{image}",
+                sums.at[image, rows_of(step)],
+                sums_recv.at[step - 1, image],
+                helper_at(step),
+            )
+
     for step in range(1, HELPERS):
-        send(f"p{step}", sums.at[:, rows_of(step)], sums_recv.at[step - 1], helper_at(step))
+        send(
+            f"w{step}",
+            cout_hbm.at[weight_piece(my_x), weight_half(core)],
+            w_all.at[HELPERS - step, weight_rows(my_x), weight_half(core)],
+            helper_at(step),
+        )
 
     over_x, over_z = pl.ds(0, ACROSS), pl.ds(ACROSS, PATCHES - ACROSS)
     arrived("x+0")
+    token(2)
     send("x++", mine.at[2, 3, 0], mine.at[2, 2, 0], east)
     arrived("x-1")
     send("x--", mine.at[2, 1, 1], mine.at[2, 2, 1], west)
@@ -281,39 +327,36 @@
     arrived("z-")
     send("z-x+", mine.at[3, 0, :, over_x], mine.at[3, 3, :, over_x], east)
     send("z-x-", mine.at[3, 0, :, over_x], mine.at[3, 1, :, over_x], west)
-    send("far", far_send, far_recv, far)
+    token(3)
     share(2, 3)
     share(2, 1)
     share(1, 0)
     share(3, 0)
 
-    arrived("p1", "p2", "p3")
-    mixed_v[...] = (
-        states_v[:, rows_of(0)].astype(F32)
-        + sums[:, rows_of(0)].astype(F32)
-        + sums_recv[0].astype(F32)
-        + sums_recv[1].astype(F32)
-        + sums_recv[2].astype(F32)
-    )
-    mixed = mixed_v[...]
-    row_mean = jnp.mean(mixed, -1, keepdims=True)
-    centred = mixed - row_mean
-    row_var = jnp.mean(centred * centred, -1, keepdims=True)
-    normed[0] = (centred * lax.rsqrt(row_var + 1e-05) * gains[1:2, :].reshape(1, 1, D)).astype(BF16)
-    for step in range(1, HELPERS):
-        send(f"n{step}", normed.at[0], normed.at[HELPERS - step], helper_at(step))
-    mixed_copy = pltpu.make_async_copy(mixed_v, mixed_out, loc_sem.at[0])
-    mixed_copy.start()
-
-    arrived("w1", "w2", "w3")
-    for step in (1, 3, 2):
-        send(
-            f"wx{step}",
-            w_out.at[pl.ds(1, 3), weight_piece(my_x), weight_half(core)],
-            w_out.at[pl.ds(1, 3), weight_piece(my_x), weight_half(core)],
-            chip_at(0, step),
-            seen=w_out.at[pl.ds(1, 3), weight_piece((my_x + X - step) % X), weight_half(core)],
+    for image in range(IMAGES):
+        arrived(*[f"p{step}{image}" for step in range(1, HELPERS)])
+        mixed = (
+            states_v[image, rows_of(0)].astype(F32)
+            + sums[image, rows_of(0)].astype(F32)
+            + sums_recv[0, image].astype(F32)
+            + sums_recv[1, image].astype(F32)
+            + sums_recv[2, image].astype(F32)
         )
+        mixed_v[image] = mixed
+        row_mean = jnp.mean(mixed, -1, keepdims=True)
+        centred = mixed - row_mean
+        row_var = jnp.mean(centred * centred, -1, keepdims=True)
+        normed[0, image] = (centred * lax.rsqrt(row_var + 1e-05) * gains[1:2, :]).astype(BF16)
+        for step in range(1, HELPERS):
+            send(
+                f"n{step}{image}",
+                normed.at[0, image],
+                normed.at[HELPERS - step, image],
+                helper_at(step),
+            )
+
+    token(4)
+    send("far", far_send, far_recv, far)
 
     @pl.loop(0, SLOTS)
     def _(m):
@@ -345,29 +388,35 @@
     send("c3", mine.at[3, 1], mine.at[4, 1], south, last_x)
     share(3, 1)
 
-    arrived("n1", "n2", "n3")
-    queries = dot_nt(normed[...].reshape(IMAGES * PATCHES, D), cproj_v[0]) * HEAD ** (-0.5)
-    q_tiles = pair_tiles(queries, None)
-    for parity in range(2):
-        for h in range(HEADS):
-            for step in range(HELPERS):
-                for image in range(IMAGES):
-                    start = ROWS * (IMAGES * step + image)
-                    qbuf[parity, image, h, rows_of(step)] = q_tiles[parity][h][start : start + ROWS]
-
-    def context_copy(pair, step):
+    arrived("w1", "w2", "w3")
+    for step in (1, 3, 2):
+        send(
+            f"wx{step}",
+            w_all.at[pl.ds(1, 3), weight_rows(my_x), weight_half(core)],
+            w_all.at[pl.ds(1, 3), weight_rows(my_x), weight_half(core)],
+            chip_at(0, step),
+            seen=w_all.at[pl.ds(1, 3), weight_rows((my_x + X - step) % X), weight_half(core)],
+        )
+
+    for image in range(IMAGES):
+        arrived(*[f"n{step}{image}" for step in range(1, HELPERS)])
+        rows = normed[:, image].reshape(PATCHES, D)
+        q_tiles = pair_tiles(dot_nt(rows, cproj_v[0]) * HEAD ** (-0.5), None)
+        for parity in range(2):
+            for h in range(HEADS):
+                for step in range(HELPERS):
+                    qbuf[parity, image, h, rows_of(step)] = q_tiles[parity][h][
+                        ROWS * step : ROWS * (step + 1)
+                    ]
+
+    def context_copy(n, step):
         return pltpu.make_async_remote_copy(
-            src_ref=ctxbuf.at[pair, rows_of(step)],
-            dst_ref=ctx_out.at[HELPERS - step, pair],
-            send_sem=c_send.at[pair, step - 1],
-            recv_sem=c_recv.at[pair, step - 1],
+            src_ref=ctxbuf.at[n, rows_of(step)],
+            dst_ref=ctx_recv.at[HELPERS - 1 - step, n],
+            send_sem=c_send.at[n, step - 1],
+            recv_sem=c_recv.at[n, step - 1],
             device_id=helper_at(step),
             device_id_type=MESH,
-        )
-
-    def own_copy(pair):
-        return pltpu.make_async_copy(
-            ctxbuf.at[pair, rows_of(0)], ctx_out.at[0, pair], own_sem.at[pair]
         )
 
     def slot_tiles(pair, parity):
@@ -383,82 +432,107 @@
             (qbuf[parity, image, h], kv[:, 128 * h : 128 * (h + 1)]) for h in range(HEADS)
         ]
 
-    def finish_pair(pair, even, odd):
+    def finish_pair(n, even, odd):
         for t, tile in enumerate(join_contexts(even, odd)):
-            ctxbuf[pair, :, 128 * t : 128 * (t + 1)] = tile
+            ctxbuf[n, :, 128 * t : 128 * (t + 1)] = tile
         for step in (2, 1, 3):
-            context_copy(pair, step).start()
-        own_copy(pair).start()
+            context_copy(n, step).start()
 
     def work_pairs(first, last):
         @pl.loop(first, last)
-        def _(pair):
+        def _(n):
+            pair = pair_at(n, my_x, core)
             contexts = head_contexts(slot_tiles(pair, 0) + slot_tiles(pair, 1))
-            finish_pair(pair, contexts[:HEADS], contexts[HEADS:])
-
-    arrived("s10", "s30")
-    work_pairs(0, 2)
+            finish_pair(n, contexts[:HEADS], contexts[HEADS:])
+
+    def y_copy(first, count):
+        return pltpu.make_async_copy(
+            y.at[pl.ds(2 * first, 2 * count)], y_out.at[pl.ds(2 * first, 2 * count)], y_sem.at[first]
+        )
+
+    def project(first, count):
+        @pl.loop(first, first + count)
+        def _(n):
+            for step in range(1, HELPERS):
+                context_copy(n, step).wait()
+
+        for parity in range(2):
+            start, weight_rows = (0, slice(PAD, None)) if parity == 0 else (128, slice(0, 256))
+            cut = slice(start, start + 256)
+            blocks = [ctxbuf[first : first + count, rows_of(0), cut]]
+            blocks += [ctx_recv[rel - 1, first : first + count, :, cut] for rel in range(1, HELPERS)]
+            lhs = jnp.concatenate([block.reshape(count * ROWS, 256) for block in blocks], axis=1)
+            rhs = jnp.concatenate([w_all[rel, weight_rows] for rel in range(HELPERS)], axis=0)
+            terms = dot(lhs, rhs)
+            for i in range(count):
+                n = first + i
+                last = n == PAIRS - 1
+                m = SLOTS - 1 if last else 2 * pair_at(n, my_x, core) + parity
+                y[2 * n + parity] = (
+                    terms[ROWS * i : ROWS * (i + 1)] + mixed_v[own_bits[m]]
+                ).astype(BF16)
+        y_copy(first, count).start()
+
+    arrived("s10", "s30", "s23", "s21")
+    work_pairs(0, 4)
     arrived("z+x-", "x-z+")
     share(1, 1)
     arrived("z-x+", "x+z-")
     share(3, 3)
-    arrived("s23", "s21", "s13", "s31", "s11", "s33")
-    work_pairs(2, 6)
-    arrived("z+x++", "x2z+")
-    share(1, 2)
-    arrived("z-x--", "x2z-")
-    share(3, 2)
-    arrived("wx1", "wx2", "wx3")
-    send(
-        "ws",
-        w_out.at[pl.ds(1, 3), :, weight_half(core)],
-        w_out.at[pl.ds(1, 3), :, weight_half(core)],
-        sibling,
-        seen=w_out.at[pl.ds(1, 3), :, weight_half(1 - core)],
-    )
-    arrived("s22", "s12", "s32")
-    work_pairs(6, 8)
-    arrived("c0", "c3")
-    share(0, 3, first_x)
-    share(4, 1, last_x)
-    arrived("s20", "s03", "s41")
-    work_pairs(8, 10)
+    arrived("s22", "s13", "s31", "s11", "s33", "s20")
+    work_pairs(4, 8)
     arrived("far")
     far_tiles = [
         (qbuf[0, own_bits[SLOTS - 1], h], far_recv[:, 128 * h : 128 * (h + 1)]) for h in range(HEADS)
     ]
     finish_pair(PAIRS - 1, head_contexts(far_tiles), None)
-
+    arrived("wx1", "wx2", "wx3")
+    send(
+        "ws",
+        w_all.at[pl.ds(1, 3), pl.ds(PAD, COLS), weight_half(core)],
+        w_all.at[pl.ds(1, 3), pl.ds(PAD, COLS), weight_half(core)],
+        sibling,
+        seen=w_all.at[pl.ds(1, 3), pl.ds(PAD, COLS), weight_half(1 - core)],
+    )
+    arrived("z+x++", "x2z+")
+    share(1, 2)
+    arrived("z-x--", "x2z-")
+    share(3, 2)
+    arrived("c0", "c3")
+    share(0, 3, first_x)
+    share(4, 1, last_x)
     arrived("ws")
     loads[4].wait()
-    mixed_copy.wait()
+    project(0, 4)
+    arrived("s12", "s32", "s03", "s41")
+    work_pairs(8, 10)
+    project(4, 4)
+    project(8, 3)
+
     for sent, _, when in copies.values():
         if when is None:
             sent().wait_send()
         else:
             pl.when(when)(lambda: sent().wait_send())
 
-    @pl.loop(0, PAIRS)
-    def _(pair):
-        for step in range(1, HELPERS):
-            context_copy(pair, step).wait()
-        own_copy(pair).wait()
-
-
-def place_kernel(
-    part, ctx_hbm, w_hbm, mixed, out, ctx, w, result, blank, places, ctx_sem, w_sem, out_sem, blank_sem
-):
+    y_copy(0, 4).wait()
+    y_copy(4, 4).wait()
+    y_copy(8, 3).wait()
+
+
+def place_kernel(part, y, out, blank, steps, out_sem):
     me = lax.axis_index("owner")
-    load_w = pltpu.make_async_copy(w_hbm, w.at[:, pl.ds(PAD, COLS)], w_sem)
-    load_ctx = pltpu.make_async_copy(ctx_hbm, ctx, ctx_sem)
-    load_w.start()
-    load_ctx.start()
-    w[:, 0:PAD] = jnp.zeros((HELPERS, PAD, D), BF16)
-    w[:, PAD + COLS :] = jnp.zeros((HELPERS, PAD, D), BF16)
     blank[...] = jnp.zeros((ROWS, D), BF16)
 
+    @pl.loop(0, PAIRS - 1)
+    def _(n):
+        steps[pair_at(n, (me // 2) % X, me % 2)] = n
+
+    def result_copy(index, image, slot):
+        return pltpu.make_async_copy(y.at[index], out.at[image, slot], out_sem.at[image, slot])
+
     def blank_copy(image, slot):
-        return pltpu.make_async_copy(blank, out.at[image, slot], blank_sem.at[image, slot])
+        return pltpu.make_async_copy(blank, out.at[image, slot], out_sem.at[image, slot])
 
     for image in range(IMAGES):
 
@@ -474,58 +548,22 @@
             pair = 2 * group + jnp.where(offset < 0, 1, 0)
             pair = jnp.where(size == 5, jnp.where(offset == 10 * (me % 2) - 5, 8, 9), pair)
             pair = jnp.where(size == 0, 9, pair)
-            index = jnp.where(size == chips // 2, SLOTS - 1, 2 * pair + parity)
-            index = jnp.clip(index, 0, SLOTS - 1)
+            index = 2 * steps[jnp.minimum(pair, 9)] + parity
+            index = jnp.where(size == chips // 2, SLOTS - 1, index)
 
             @pl.when(p >= 0)
             def _():
-                places[index] = image * SLOTS + slot
+                result_copy(index, image, slot).start()
 
             @pl.when(p < 0)
             def _():
                 blank_copy(image, slot).start()
 
-    load_w.wait()
-    load_ctx.wait()
-
-    def out_copy(index):
-        place = places[index]
-        return pltpu.make_async_copy(
-            result.at[index],
-            out.at[lax.div(place, SLOTS), lax.rem(place, SLOTS)],
-            out_sem.at[index],
-        )
-
-    for first, count in ((0, 6), (6, 5)):
-        for parity in range(2):
-            start, weight_rows = (0, slice(PAD, None)) if parity == 0 else (128, slice(0, 256))
-            lhs = jnp.concatenate(
-                [
-                    ctx[h, first : first + count, :, start : start + 256].reshape(count * ROWS, 256)
-                    for h in range(HELPERS)
-                ],
-                axis=1,
-            )
-            rhs = jnp.concatenate([w[h, weight_rows] for h in range(HELPERS)], axis=0)
-            terms = dot(lhs, rhs)
-            for n in range(count):
-                index = 2 * (first + n) + parity
-                if index < SLOTS:
-                    image = lax.div(places[index], SLOTS)
-                    result[index] = (terms[ROWS * n : ROWS * (n + 1)] + mixed[image]).astype(BF16)
-                    out_copy(index).start()
-
-    @pl.loop(0, SLOTS)
-    def _(index):
-        out_copy(index).wait()
-
     for image in range(IMAGES):
 
         @pl.loop(0, SLOTS)
         def _(slot):
-            @pl.when(part[image, slot] < 0)
-            def _():
-                blank_copy(image, slot).wait()
+            blank_copy(image, slot).wait()
 
 
 def local(states, partners, self_proj, self_out, cross_proj, cross_out, gains):
@@ -533,15 +571,11 @@
     smem = pl.BlockSpec(memory_space=pltpu.SMEM)
     vmem = pl.BlockSpec(memory_space=pltpu.VMEM)
     dma = pltpu.SemaphoreType.DMA
-    ctx, weight, mixed = pl.pallas_call(
+    y = pl.pallas_call(
         exchange_kernel,
-        out_shape=(
-            jax.ShapeDtypeStruct((HELPERS, PAIRS, ROWS, LANES), BF16),
-            jax.ShapeDtypeStruct((HELPERS, COLS, D), BF16),
-            jax.ShapeDtypeStruct((IMAGES, ROWS, D), F32),
-        ),
+        out_shape=jax.ShapeDtypeStruct((2 * PAIRS, ROWS, D), BF16),
         in_specs=[smem, any_spec, any_spec, any_spec, any_spec, any_spec, vmem],
-        out_specs=(any_spec, any_spec, any_spec),
+        out_specs=any_spec,
         scratch_shapes=[
             pltpu.VMEM((IMAGES, PATCHES, D), BF16),
             pltpu.VMEM((3, COLS, D), BF16),
@@ -559,11 +593,14 @@
             pltpu.VMEM((HELPERS, IMAGES, ROWS, D), BF16),
             pltpu.VMEM((2, IMAGES, HEADS, PATCHES, 2 * HEAD), BF16),
             pltpu.VMEM((PAIRS, PATCHES, LANES), BF16),
+            pltpu.VMEM((HELPERS - 1, PAIRS, ROWS, LANES), BF16),
+            pltpu.VMEM((HELPERS, COLS + 2 * PAD, D), BF16),
+            pltpu.VMEM((2 * PAIRS, ROWS, D), BF16),
             pltpu.SMEM((SLOTS,), jnp.int32),
             pltpu.SMEM((SLOTS,), jnp.int32),
             dma((5,)),
-            dma((1,)),
             dma((PAIRS,)),
+            pltpu.SemaphoreType.REGULAR((3,)),
             dma((COPIES,)),
             dma((COPIES,)),
             dma((PAIRS, 3)),
@@ -585,22 +622,16 @@
     return pl.pallas_call(
         place_kernel,
         out_shape=jax.ShapeDtypeStruct((IMAGES, SLOTS, ROWS, D), BF16),
-        in_specs=[smem, any_spec, any_spec, vmem],
+        in_specs=[smem, vmem],
         out_specs=any_spec,
         scratch_shapes=[
-            pltpu.VMEM((HELPERS, PAIRS, ROWS, LANES), BF16),
-            pltpu.VMEM((HELPERS, COLS + 2 * PAD, D), BF16),
-            pltpu.VMEM((SLOTS, ROWS, D), BF16),
             pltpu.VMEM((ROWS, D), BF16),
-            pltpu.SMEM((SLOTS,), jnp.int32),
-            dma,
-            dma,
-            dma((SLOTS,)),
+            pltpu.SMEM((PAIRS,), jnp.int32),
             dma((IMAGES, SLOTS)),
         ],
         compiler_params=pltpu.CompilerParams(vmem_limit_bytes=VMEM_LIMIT),
         name="place",
-    )(partners, ctx, weight, mixed)
+    )(partners, y)
 
 
 def solution(mesh):

time: 48.5 us -> 46.6 us (0.961)
  Pallas kernels: 47.9 us -> 46.4 us
    pallas_call x1, Pallas kernels: 5.56 us -> 3.9 us  [local(): pl.pallas_call(place_kernel, out_shape=jax.ShapeDtypeStruct((IMAGES, SLOT...]
where the time goes in v4:
time: 46.6 us; the launch traced here: 46.4 us
  Pallas kernels  46.4 us (100%)
    pallas_call x1, Pallas kernels, local(): pl.pallas_call(exchange_kernel, out_shape=jax.ShapeDtypeStruct((2 * PAIRS...  42.5 us
    pallas_call x1, Pallas kernels, local(): pl.pallas_call(place_kernel, out_shape=jax.ShapeDtypeStruct((IMAGES, SLOT...  3.9 us

profile of v4, /device:TPU:1, one launch (start us, length us, event | category | flops | bytes accessed | tf_op | source)
XLA Modules:
  0.0 46.4 jit_solution(10797412196104957970)
XLA Ops:
  0.0 42.5 %exchange.1.y = bf16[22,32,768]{2,1,0:T(8,128)(2,1)} custom-call(s32[2,21]{1,0:T(2,128)} %part.3, bf16[2,128,768]{2,1,0:T(8,128)(2,1)} %states_hbm.1, bf16[3,192,768]{2,1,0:T(8,128)(2,1)} %bitcast.2, bf16[192,768]{1,0:T(8,128)(2,1)} %sout_hbm.1, bf16[3,192,768]{2,1,0:T(8,128)(2,1)} %bitcast.3, bf16[192,768]{1,0:T(8,128)(2,1)} %cout_hbm.1, f32[3,768]{1,0:T(4,128)} %gains.1), custom_call_target="tpu_custom_call" | custom-call | tf_op jit(solution)/shard_map/exchange/pallas_call | solution.py:574
  42.5 3.9 %place.1 = bf16[2,21,32,768]{3,2,1,0:T(8,128)(2,1)} custom-call(s32[2,21]{1,0:T(2,128)} %part.3, bf16[22,32,768]{2,1,0:T(8,128)(2,1)} %exchange.1.y), custom_call_target="tpu_custom_call" | custom-call | tf_op jit(solution)/shard_map/place/pallas_call | solution.py:622

commit v5 on v4

--- a/solution.py
+++ b/solution.py
@@ -281,6 +281,7 @@
     def rows_of(step):
         return pl.ds(pl.multiple_of(((my_h + step) % HELPERS) * ROWS, ROWS), ROWS)
 
+    token(2)
     loads[3].wait()
     for image in range(IMAGES):
         piece = slice(PATCHES * image, PATCHES * (image + 1))
@@ -310,8 +311,8 @@
         )
 
     over_x, over_z = pl.ds(0, ACROSS), pl.ds(ACROSS, PATCHES - ACROSS)
+    token(3)
     arrived("x+0")
-    token(2)
     send("x++", mine.at[2, 3, 0], mine.at[2, 2, 0], east)
     arrived("x-1")
     send("x--", mine.at[2, 1, 1], mine.at[2, 2, 1], west)
@@ -321,13 +322,14 @@
     arrived("x-0")
     send("x-z+", mine.at[2, 1, :, over_z], mine.at[1, 1, :, over_z], north)
     send("x-z-", mine.at[2, 1, :, over_z], mine.at[3, 1, :, over_z], south)
+    token(4)
+    send("far", far_send, far_recv, far)
     arrived("z+")
     send("z+x+", mine.at[1, 0, :, over_x], mine.at[1, 3, :, over_x], east)
     send("z+x-", mine.at[1, 0, :, over_x], mine.at[1, 1, :, over_x], west)
     arrived("z-")
     send("z-x+", mine.at[3, 0, :, over_x], mine.at[3, 3, :, over_x], east)
     send("z-x-", mine.at[3, 0, :, over_x], mine.at[3, 1, :, over_x], west)
-    token(3)
     share(2, 3)
     share(2, 1)
     share(1, 0)
@@ -355,9 +357,25 @@
                 helper_at(step),
             )
 
-    token(4)
-    send("far", far_send, far_recv, far)
-
+    arrived("w1", "w2", "w3")
+    for step in (1, 3, 2):
+        send(
+            f"wx{step}",
+            w_all.at[pl.ds(1, 3), weight_rows(my_x), weight_half(core)],
+            w_all.at[pl.ds(1, 3), weight_rows(my_x), weight_half(core)],
+            chip_at(0, step),
+            seen=w_all.at[pl.ds(1, 3), weight_rows((my_x + X - step) % X), weight_half(core)],
+        )
+
+    arrived("x--", "x++")
+    send("x2z+", mine.at[2, 2, :, over_z], mine.at[1, 2, :, over_z], north)
+    send("x2z-", mine.at[2, 2, :, over_z], mine.at[3, 2, :, over_z], south)
+    share(2, 2)
+    first_x, last_x = my_x == 0, my_x == X - 1
+    arrived("x+z+")
+    send("c0z", mine.at[1, 3, :, over_z], mine.at[0, 3, :, over_z], north, first_x)
+    arrived("x-z-")
+    send("c3z", mine.at[3, 1, :, over_z], mine.at[4, 1, :, over_z], south, last_x)
     @pl.loop(0, SLOTS)
     def _(m):
         offset, layer = slot_owner(m // 2, m % 2, core)
@@ -372,32 +390,14 @@
         own_bits[m] = code // 2
         partner_bits[m] = code % 2
 
-    arrived("x--", "x++")
-    send("x2z+", mine.at[2, 2, :, over_z], mine.at[1, 2, :, over_z], north)
-    send("x2z-", mine.at[2, 2, :, over_z], mine.at[3, 2, :, over_z], south)
-    share(2, 2)
     arrived("z+x+")
     send("z+x++", mine.at[1, 3, :, over_x], mine.at[1, 2, :, over_x], east)
+    send("c0x", mine.at[1, 3, :, over_x], mine.at[0, 3, :, over_x], north, first_x)
     arrived("z-x-")
     send("z-x--", mine.at[3, 1, :, over_x], mine.at[3, 2, :, over_x], west)
-    first_x, last_x = my_x == 0, my_x == X - 1
-    arrived("x+z+")
-    send("c0", mine.at[1, 3], mine.at[0, 3], north, first_x)
+    send("c3x", mine.at[3, 1, :, over_x], mine.at[4, 1, :, over_x], south, last_x)
     share(1, 3)
-    arrived("x-z-")
-    send("c3", mine.at[3, 1], mine.at[4, 1], south, last_x)
     share(3, 1)
-
-    arrived("w1", "w2", "w3")
-    for step in (1, 3, 2):
-        send(
-            f"wx{step}",
-            w_all.at[pl.ds(1, 3), weight_rows(my_x), weight_half(core)],
-            w_all.at[pl.ds(1, 3), weight_rows(my_x), weight_half(core)],
-            chip_at(0, step),
-            seen=w_all.at[pl.ds(1, 3), weight_rows((my_x + X - step) % X), weight_half(core)],
-        )
-
     for image in range(IMAGES):
         arrived(*[f"n{step}{image}" for step in range(1, HELPERS)])
         rows = normed[:, image].reshape(PATCHES, D)
@@ -498,7 +498,7 @@
     share(1, 2)
     arrived("z-x--", "x2z-")
     share(3, 2)
-    arrived("c0", "c3")
+    arrived("c0z", "c3z", "c0x", "c3x")
     share(0, 3, first_x)
     share(4, 1, last_x)
     arrived("ws")

time: 46.6 us -> 45.3 us (0.972)
  Pallas kernels: 46.4 us -> 45 us
    pallas_call x1, Pallas kernels: 42.5 us -> 41.1 us  [local(): pl.pallas_call(exchange_kernel, out_shape=jax.ShapeDtypeStruct((2 * PAIRS...]
where the time goes in v5:
time: 45.3 us; the launch traced here: 45 us
  Pallas kernels  45 us (99%)
    pallas_call x1, Pallas kernels, local(): pl.pallas_call(exchange_kernel, out_shape=jax.ShapeDtypeStruct((2 * PAIRS...  41.1 us
    pallas_call x1, Pallas kernels, local(): pl.pallas_call(place_kernel, out_shape=jax.ShapeDtypeStruct((IMAGES, SLOT...  3.9 us

profile of v5, /device:TPU:1, one launch (start us, length us, event | category | flops | bytes accessed | tf_op | source)
XLA Modules:
  0.0 45.0 jit_solution(15991700673521516925)
XLA Ops:
  0.0 41.1 %exchange.1.y = bf16[22,32,768]{2,1,0:T(8,128)(2,1)} custom-call(s32[2,21]{1,0:T(2,128)} %part.3, bf16[2,128,768]{2,1,0:T(8,128)(2,1)} %states_hbm.1, bf16[3,192,768]{2,1,0:T(8,128)(2,1)} %bitcast.2, bf16[192,768]{1,0:T(8,128)(2,1)} %sout_hbm.1, bf16[3,192,768]{2,1,0:T(8,128)(2,1)} %bitcast.3, bf16[192,768]{1,0:T(8,128)(2,1)} %cout_hbm.1, f32[3,768]{1,0:T(4,128)} %gains.1), custom_call_target="tpu_custom_call" | custom-call | tf_op jit(solution)/shard_map/exchange/pallas_call | solution.py:574
  41.1 3.9 %place.1 = bf16[2,21,32,768]{3,2,1,0:T(8,128)(2,1)} custom-call(s32[2,21]{1,0:T(2,128)} %part.3, bf16[22,32,768]{2,1,0:T(8,128)(2,1)} %exchange.1.y), custom_call_target="tpu_custom_call" | custom-call | tf_op jit(solution)/shard_map/place/pallas_call | solution.py:622

commit v6 on v5

--- a/solution.py
+++ b/solution.py
@@ -467,6 +467,9 @@
             for i in range(count):
                 n = first + i
                 last = n == PAIRS - 1
+                if last and parity == 1:
+                    y[SLOTS] = jnp.zeros((ROWS, D), BF16)
+                    continue
                 m = SLOTS - 1 if last else 2 * pair_at(n, my_x, core) + parity
                 y[2 * n + parity] = (
                     terms[ROWS * i : ROWS * (i + 1)] + mixed_v[own_bits[m]]
@@ -520,9 +523,8 @@
     y_copy(8, 3).wait()
 
 
-def place_kernel(part, y, out, blank, steps, out_sem):
+def place_kernel(part, y, out, steps, out_sem):
     me = lax.axis_index("owner")
-    blank[...] = jnp.zeros((ROWS, D), BF16)
 
     @pl.loop(0, PAIRS - 1)
     def _(n):
@@ -531,12 +533,9 @@
     def result_copy(index, image, slot):
         return pltpu.make_async_copy(y.at[index], out.at[image, slot], out_sem.at[image, slot])
 
-    def blank_copy(image, slot):
-        return pltpu.make_async_copy(blank, out.at[image, slot], out_sem.at[image, slot])
-
     for image in range(IMAGES):
 
-        @pl.loop(0, SLOTS)
+        @pl.loop(0, SLOTS, unroll=7)
         def _(slot):
             p = part[image, slot]
             owner = lax.div(jnp.maximum(p, 0), 2)
@@ -551,19 +550,14 @@
             index = 2 * steps[jnp.minimum(pair, 9)] + parity
             index = jnp.where(size == chips // 2, SLOTS - 1, index)
 
-            @pl.when(p >= 0)
-            def _():
-                result_copy(index, image, slot).start()
-
-            @pl.when(p < 0)
-            def _():
-                blank_copy(image, slot).start()
+            index = jnp.where(p >= 0, index, SLOTS)
+            result_copy(index, image, slot).start()
 
     for image in range(IMAGES):
 
-        @pl.loop(0, SLOTS)
+        @pl.loop(0, SLOTS, unroll=7)
         def _(slot):
-            blank_copy(image, slot).wait()
+            result_copy(0, image, slot).wait()
 
 
 def local(states, partners, self_proj, self_out, cross_proj, cross_out, gains):
@@ -625,7 +619,6 @@
         in_specs=[smem, vmem],
         out_specs=any_spec,
         scratch_shapes=[
-            pltpu.VMEM((ROWS, D), BF16),
             pltpu.SMEM((PAIRS,), jnp.int32),
             dma((IMAGES, SLOTS)),
         ],

time: 45.3 us -> 44.7 us (0.987)
  Pallas kernels: 45 us -> 44.4 us
    pallas_call x1, Pallas kernels: 3.9 us -> 3.35 us  [local(): pl.pallas_call(place_kernel, out_shape=jax.ShapeDtypeStruct((IMAGES, SLOT...]
where the time goes in v6:
time: 44.7 us; the launch traced here: 44.4 us
  Pallas kernels  44.4 us (99%)
    pallas_call x1, Pallas kernels, local(): pl.pallas_call(exchange_kernel, out_shape=jax.ShapeDtypeStruct((2 * PAIRS...  41.1 us
    pallas_call x1, Pallas kernels, local(): pl.pallas_call(place_kernel, out_shape=jax.ShapeDtypeStruct((IMAGES, SLOT...  3.35 us

profile of v6, /device:TPU:1, one launch (start us, length us, event | category | flops | bytes accessed | tf_op | source)
XLA Modules:
  0.0 44.4 jit_solution(2728988434443509966)
XLA Ops:
  0.0 41.1 %exchange.1.y = bf16[22,32,768]{2,1,0:T(8,128)(2,1)} custom-call(s32[2,21]{1,0:T(2,128)} %part.3, bf16[2,128,768]{2,1,0:T(8,128)(2,1)} %states_hbm.1, bf16[3,192,768]{2,1,0:T(8,128)(2,1)} %bitcast.2, bf16[192,768]{1,0:T(8,128)(2,1)} %sout_hbm.1, bf16[3,192,768]{2,1,0:T(8,128)(2,1)} %bitcast.3, bf16[192,768]{1,0:T(8,128)(2,1)} %cout_hbm.1, f32[3,768]{1,0:T(4,128)} %gains.1), custom_call_target="tpu_custom_call" | custom-call | tf_op jit(solution)/shard_map/exchange/pallas_call | solution.py:568
  41.1 3.3 %place.1 = bf16[2,21,32,768]{3,2,1,0:T(8,128)(2,1)} custom-call(s32[2,21]{1,0:T(2,128)} %part.3, bf16[22,32,768]{2,1,0:T(8,128)(2,1)} %exchange.1.y), custom_call_target="tpu_custom_call" | custom-call | tf_op jit(solution)/shard_map/place/pallas_call | solution.py:616
